TPU v7x, 128 devices: a whole 4x4x4 slice. The times are simulated.
128 devices in a mesh: group: 8 (over z, core), member: 16 (over x, y).
Axes of the slice: x: 4, y: 4, z: 4, core: 2. Of those that a mesh axis runs over, the one named last changes fastest.
Arguments:
- dense_in: float32 [16384, 13], P(('group', 'member')), may hold values from -6 to 6
- lookup_owner: int32 [16384, 8, 8], P(('group', 'member')), may hold values from 0 to 127, as said below
- lookup_row: int32 [16384, 8, 8], P(('group', 'member')), may hold values from 0 to 8191
- bag_length: int32 [16384, 8], P(('group', 'member')), may hold values from 1 to 8
- logit_grad: float32 [16384], P(('group', 'member')), may hold values from -6 to 6
- table: float32 [1048576, 128], P(('group', 'member')), may hold values from -1.2 to 1.2
- parity: float32 [65536, 256], P(('group', 'member')), may hold values from -3 to 3
- w_bottom0: float32 [13, 512], replicated, may hold values from -1.75 to 1.75
- w_bottom1: float32 [512, 256], replicated, may hold values from -0.25 to 0.25
- w_bottom2: float32 [256, 128], replicated, may hold values from -0.375 to 0.375
- w_top0: float32 [164, 1024], replicated, may hold values from -0.5 to 0.5
- w_top1: float32 [1024], replicated, may hold values from -0.1875 to 0.1875
Outputs:
- new_table: float32 [1048576, 128], P(('group', 'member'))
- new_parity: float32 [65536, 256], P(('group', 'member'))
- grad_bottom0: float32 [13, 512], replicated
- grad_bottom1: float32 [512, 256], replicated
- grad_bottom2: float32 [256, 128], replicated
- grad_top0: float32 [164, 1024], replicated
- grad_top1: float32 [1024], replicated
Inputs may be any that keep to these rules, and one draw needn't show every extreme that they name: `lookup_owner`: among the 8192 bag slots of one device's samples at most 97 name rows of any one device, and one device is named by exactly 97 slots of every device. `bag_length`: slots at or beyond a bag's length are padding; their owner and row are still in range.
All inputs are finite; a program needn't handle non-finite values.
Results may differ from a plain program's by a relative error of at most 0.005.
Values may be sent and summed in bfloat16 or wider, within the bound.
A program may use at most 128 MiB of HBM per device.

v0:
```python
import jax
import jax.numpy as jnp
import numpy as np
from jax import lax
from jax.sharding import PartitionSpec as P

embed_rate = 1.0


def network(w_bottom0, w_bottom1, w_bottom2, w_top0, w_top1, pooled, dense_in):
    highest = lax.Precision.HIGHEST
    hidden_one = jax.nn.silu(jnp.dot(dense_in, w_bottom0, precision=highest))
    hidden_two = jax.nn.silu(jnp.dot(hidden_one, w_bottom1, precision=highest))
    bottom = jax.nn.silu(jnp.dot(hidden_two, w_bottom2, precision=highest))
    stacked = jnp.concatenate([bottom[:, None, :], pooled], axis=1)
    gram_dots = jnp.einsum("sie,sje->sij", stacked, stacked, precision=highest)
    lower_rows, lower_cols = np.tril_indices(stacked.shape[1], -1)
    pair_dots = gram_dots[:, lower_rows, lower_cols]
    top_in = jnp.concatenate([bottom, pair_dots], axis=1)
    hidden = jax.nn.silu(jnp.dot(top_in, w_top0, precision=highest))
    return jnp.dot(hidden, w_top1, precision=highest)


def body(
    dense_in,
    lookup_owner,
    lookup_row,
    bag_length,
    logit_grad,
    table,
    parity,
    w_bottom0,
    w_bottom1,
    w_bottom2,
    w_top0,
    w_top1,
):
    shards = lax.axis_size(("group", "member"))
    members = lax.axis_size("member")
    samples, tables, bag_slots = lookup_owner.shape
    feature_width = table.shape[1]
    lookups = samples * tables * bag_slots
    capacity = max(3 * lookups // (2 * shards) + 1, 2)
    owner_flat = lookup_owner.reshape(-1)
    row_flat = lookup_row.reshape(-1)
    matches = (owner_flat[:, None] == jnp.arange(shards, dtype=jnp.int32)[None, :]).astype(
        jnp.int32
    )
    before = jnp.cumsum(matches, axis=0) - matches
    position = jnp.sum(before * matches, axis=1)
    target = owner_flat * capacity + position
    send_ids = (
        jnp.zeros((shards * capacity,), jnp.int32)
        .at[target]
        .set(row_flat)
        .reshape(shards, capacity)
    )
    served_ids = lax.all_to_all(
        send_ids, ("group", "member"), split_axis=0, concat_axis=0, tiled=True
    )
    served_rows = jnp.take(table, served_ids, axis=0).astype(jnp.bfloat16)
    fetched = lax.all_to_all(
        served_rows, ("group", "member"), split_axis=0, concat_axis=0, tiled=True
    )
    gathered = fetched.reshape(shards * capacity, feature_width)[target]
    gathered = gathered.reshape(samples, tables, bag_slots, feature_width)
    live_mask = (
        jnp.arange(bag_slots, dtype=jnp.int32)[None, None, :] < bag_length[:, :, None]
    ).astype(jnp.bfloat16)
    pooled = jnp.einsum("sthe,sth->ste", gathered, live_mask, preferred_element_type=jnp.float32)

    def forward(first_w, second_w, third_w, top_first, top_second, pooled_in):
        return network(first_w, second_w, third_w, top_first, top_second, pooled_in, dense_in)

    logits, pullback = jax.vjp(forward, w_bottom0, w_bottom1, w_bottom2, w_top0, w_top1, pooled)
    gradients = pullback(logit_grad)
    dense_grads = lax.psum(
        (gradients[0], gradients[1], gradients[2], gradients[3], gradients[4]), ("group", "member")
    )
    pooled_grad = gradients[5].astype(jnp.bfloat16)
    lookup_grad = (pooled_grad[:, :, None, :] * live_mask[:, :, :, None]).reshape(
        lookups, feature_width
    )
    send_grads = (
        jnp.zeros((shards * capacity, feature_width), jnp.bfloat16).at[target].set(lookup_grad)
    )
    received = lax.all_to_all(
        send_grads.reshape(shards, capacity, feature_width),
        ("group", "member"),
        split_axis=0,
        concat_axis=0,
        tiled=True,
    )
    row_grad = (
        jnp.zeros(table.shape, jnp.float32)
        .at[served_ids.reshape(-1)]
        .add(received.reshape(-1, feature_width).astype(jnp.float32))
    )
    new_table = table - embed_rate * row_grad
    change = -embed_rate * row_grad
    piece_rows = table.shape[0] // members
    pieces = lax.all_to_all(
        change.reshape(members, piece_rows, feature_width),
        "member",
        split_axis=0,
        concat_axis=0,
        tiled=True,
    )
    sources = jnp.arange(members, dtype=jnp.float32) / members
    coeffs = 1.0 / (1.0 + jnp.arange(2, dtype=jnp.float32)[:, None] + sources[None, :])
    update = jnp.einsum("mre,km->rke", pieces, coeffs, precision=lax.Precision.HIGHEST).reshape(
        piece_rows, 2 * feature_width
    )
    new_parity = parity + update
    return (
        new_table,
        new_parity,
        dense_grads[0],
        dense_grads[1],
        dense_grads[2],
        dense_grads[3],
        dense_grads[4],
    )


def solution(mesh):
    in_specs = (
        P(("group", "member"), None),
        P(("group", "member"), None, None),
        P(("group", "member"), None, None),
        P(("group", "member"), None),
        P(("group", "member")),
        P(("group", "member"), None),
        P(("group", "member"), None),
        P(),
        P(),
        P(),
        P(),
        P(),
    )
    out_specs = (
        P(("group", "member"), None),
        P(("group", "member"), None),
        P(),
        P(),
        P(),
        P(),
        P(),
    )
    return jax.shard_map(body, mesh=mesh, in_specs=in_specs, out_specs=out_specs, check_vma=False)
```

profile of v0, /device:TPU:1, one launch (start us, length us, event | category | flops | bytes accessed | tf_op | source)
XLA Modules:
  0.0 593.0 jit_solution(2511284512159685374)
XLA Ops:
  10.8 2.0 copy-done.2
  12.9 2.6 broadcast_add_fusion
  15.5 4.4 copy.50
  21.0 4.4 fusion.1
  25.5 30.5 %scatter_custom_fusion = s32[12416]{0:T(1024)S(1)} fusion(s32[8192]{0:T(1024)S(1)} %bitcast.75, s32[8192]{0:T(1024)S(1)} %reshape.211, s32[]{:T(128)} %constant.18.clone.1), kind=kCustom, calls=%fused_computation.79 | custom fusion | bytes 49668 | tf_op jit(solution)/shard_map/scatter | solution.py:55
  56.2 20.9 %all_to_all.30 = s32[128,1,97]{2,1,0:T(1,128)S(1)} all-to-all(s32[128,1,97]{2,1,0:T(1,128)S(1)} %bitcast.73), channel_id=1, replica_groups=mesh['group'=8,'member'=16] {'group','member'}, dimensions={0} | all-to-all | bytes 99328 | tf_op jit(solution)/shard_map/all_to_all | solution.py:58
  77.3 26.0 %gather_fusion = bf16[12416,128]{1,0:T(8,128)(2,1)} fusion(f32[8192,128]{1,0:T(8,128)} %param.21, s32[13312]{0:T(1024)S(1)} %pad_clamp_fusion), kind=kCustom, calls=%fused_computation | custom fusion | bytes 6406656 | tf_op jit(solution)/shard_map/jit(_take)/gather | solution.py:61
  103.3 5.5 reshape.186
  108.9 7.1 %select_convert_fusion = bf16[128,97,128]{2,1,0:T(8,128)(2,1)} fusion(bf16[128,97,128]{2,1,0:T(8,128)(2,1)} %reshape.186, pred[128,97]{1,0:T(8,128)(4,1)S(1)} %compare_and_fusion), kind=kLoop, calls=%fused_computation.7 | loop fusion | flops 1589248 | bytes 6369408 | tf_op jit(solution)/shard_map/convert_element_type | solution.py:61
  116.0 6.1 %all-to-all-start.1 = ((bf16[128,97,128]{2,1,0:T(8,128)(2,1)}), bf16[128,97,128]{2,1,0:T(8,128)(2,1)}, u32[]{:S(2)}, u32[]{:S(2)}) async-start(bf16[128,97,128]{2,1,0:T(8,128)(2,1)} %select_convert_fusion), calls=%async_computation.1 | async-start | bytes 6815744 | tf_op jit(solution)/shard_map/all_to_all | solution.py:62
  124.8 41.2 %all-to-all-done.1 = bf16[128,97,128]{2,1,0:T(8,128)(2,1)} async-done(((bf16[128,97,128]{2,1,0:T(8,128)(2,1)}), bf16[128,97,128]{2,1,0:T(8,128)(2,1)}, u32[]{:S(2)}, u32[]{:S(2)}) %all-to-all-start.1) | async-done | bytes 3178528 | tf_op jit(solution)/shard_map/all_to_all | solution.py:62
  165.9 5.5 reshape.178
  171.5 30.3 %gather_fusion.1 = bf16[8192,128]{1,0:T(8,128)(2,1)} fusion(bf16[12416,128]{1,0:T(8,128)(2,1)} %reshape.178, s32[8192]{0:T(1024)S(1)} %broadcast_clamp_fusion), kind=kCustom, calls=%fused_computation.1 | custom fusion | bytes 4227072 | tf_op jit(solution)/shard_map/gather | solution.py:65
  201.8 2.8 fusion.9
  204.7 1.8 fusion.15
  209.9 3.6 scatter_fusion
  214.0 2.2 fusion.13
  216.2 1.9 fusion.14
  221.4 23.3 %scatter_custom_fusion.2 = bf16[12416,128]{1,0:T(8,128)(2,1)} fusion(s32[8192]{0:T(1024)} %bitcast.77, bf16[8192,128]{1,0:T(8,128)(2,1)S(1)} %bitcast_multiply_fusion, bf16[]{:T(256)} %constant.23.clone.1), kind=kCustom, calls=%fused_computation.25 | custom fusion | bytes 3179008 | tf_op jit(solution)/shard_map/scatter | solution.py:85
  244.7 5.5 reshape.180
  250.2 5.1 all-to-all-start.2
  257.0 42.0 %all-to-all-done.2 = bf16[128,97,128]{2,1,0:T(8,128)(2,1)} async-done(((bf16[128,97,128]{2,1,0:T(8,128)(2,1)}), bf16[128,97,128]{2,1,0:T(8,128)(2,1)}, u32[]{:S(2)}, u32[]{:S(2)}) %all-to-all-start.2) | async-done | bytes 3178528 | tf_op jit(solution)/shard_map/all_to_all | solution.py:87
  299.0 6.0 %reshape.233 = f32[12416,128]{1,0:T(8,128)} reshape(bf16[128,97,128]{2,1,0:T(8,128)(2,1)} %all-to-all-done.2) | data formatting | bytes 9535488 | tf_op jit(solution)/shard_map/convert_element_type | solution.py:97
  305.0 74.7 %scatter_custom_fusion.3 = f32[8192,128]{1,0:T(8,128)} fusion(s32[12416]{0:T(1024)S(1)} %fusion.39, f32[12416,128]{1,0:T(8,128)} %reshape.233, f32[]{:T(128)} %constant.17.clone.1), kind=kCustom, calls=%fused_computation.21 | custom fusion | flops 1589248 | bytes 4194816 | tf_op jit(solution)/shard_map/scatter-add | solution.py:97
  379.7 7.4 %broadcast_multiply_fusion = (f32[8192,128]{1,0:T(8,128)}, f32[8192,128]{1,0:T(8,128)}) fusion(f32[8192,128]{1,0:T(8,128)} %scatter_custom_fusion.3, f32[8192,128]{1,0:T(8,128)} %param.21), kind=kLoop, calls=%fused_computation.18 | loop fusion | flops 2097152 | bytes 16777216 | tf_op jit(solution)/shard_map/mul | solution.py:100
  387.1 4.7 all-to-all-start.3
  394.8 1.8 fusion.33
  398.2 117.1 %all-reduce = (f32[13,512]{1,0:T(8,128)}, f32[1024]{0:T(1024)}) all-reduce(f32[13,512]{1,0:T(8,128)S(1)} %convolution_bitcast_fusion, f32[1024]{0:T(1024)S(1)} %bitcast.78), channel_id=1, replica_groups=mesh['group'=8,'member'=16] {'group','member'}, use_global_device_ids=true, to_apply=%region_7.8 | all-reduce | flops 7680 | bytes 61440 | tf_op jit(solution)/shard_map/psum | solution.py:77
  515.3 6.4 %fusion.2 = f32[2,512,128]{2,0,1:T(2,128)S(1)} fusion(f32[16,512,128]{2,1,0:T(8,128)} %all-to-all-done.3, f32[16]{0:T(128)S(1)} %iota_multiply_fusion, f32[2]{0:T(128)S(1)} %iota_add_fusion), kind=kOutput, calls=%fused_computation.11 | convolution fusion | flops 25165888 | bytes 4718664 | tf_op jit(solution)/shard_map/mre,km->rke/dot_general | solution.py:111
  522.6 57.9 %all-reduce.4.cloned.1.call-done = (f32[512,256]{1,0:T(8,128)}, f32[256,128]{1,0:T(8,128)}, f32[164,1024]{1,0:T(8,128)}) async-done(((f32[512,256]{1,0:T(8,128)}, f32[256,128]{1,0:T(8,128)}, f32[164,1024]{1,0:T(8,128)}), (f32[512,256]{1,0:T(8,128)}, f32[256,128]{1,0:T(8,128)}, f32[164,1024]{1,0:T(8,128)})) %all-reduce.4.cloned.1.call-update) | async-done | bytes 1327120 | tf_op jit(solution)/shard_map/psum | solution.py:77
  580.5 1.9 copy.74
  584.0 2.0 copy.76
  (111 shorter events, 23.6 us)
Async XLA Ops:
  7.2 200.5 %copy-start = (f32[164,1024]{1,0:T(8,128)S(1)}, f32[164,1024]{1,0:T(8,128)}, u32[]{:S(2)}) copy-start(f32[164,1024]{1,0:T(8,128)} %param.26) | copy-start | bytes 2015236
  10.8 2.0 copy-start.2
  15.5 5.0 copy-start.20
  25.5 99.2 %copy-start.15 = (s32[8192,1]{0,1:T(1,128)}, s32[8192,1]{0,1:T(1,128)S(1)}, u32[]{:S(2)}) copy-start(s32[8192,1]{0,1:T(1,128)S(1)} %compare_select_fusion.1) | copy-start | bytes 98308
  116.0 6.1 %copy-start.23 = (s32[128,8]{0,1:T(8,128)S(1)}, s32[128,8]{0,1:T(8,128)}, u32[]{:S(2)}) copy-start(s32[128,8]{0,1:T(8,128)} %param.19) | copy-start | bytes 12292
  116.0 6.2 %copy-start.21 = (f32[13,512]{1,0:T(8,128)S(1)}, f32[13,512]{1,0:T(8,128)}, u32[]{:S(2)}) copy-start(f32[13,512]{1,0:T(8,128)} %param.23) | copy-start | bytes 79876
  116.0 6.2 %copy-start.22 = (f32[128,13]{0,1:T(8,128)S(1)}, f32[128,13]{0,1:T(8,128)}, u32[]{:S(2)}) copy-start(f32[128,13]{0,1:T(8,128)} %param.16) | copy-start | bytes 19972
  116.0 6.7 %copy-start.5 = (f32[512,256]{1,0:T(8,128)S(1)}, f32[512,256]{1,0:T(8,128)}, u32[]{:S(2)}) copy-start(f32[512,256]{1,0:T(8,128)} %param.24) | copy-start | bytes 1572868
  116.0 7.1 %copy-start.13 = (f32[256,128]{1,0:T(8,128)S(1)}, f32[256,128]{1,0:T(8,128)}, u32[]{:S(2)}) copy-start(f32[256,128]{1,0:T(8,128)} %param.25) | copy-start | bytes 393220
  116.0 49.9 %all-to-all-start.1 = ((bf16[128,97,128]{2,1,0:T(8,128)(2,1)}), bf16[128,97,128]{2,1,0:T(8,128)(2,1)}, u32[]{:S(2)}, u32[]{:S(2)}) async-start(bf16[128,97,128]{2,1,0:T(8,128)(2,1)} %select_convert_fusion), calls=%async_computation.1 | async-start | bytes 6815744 | tf_op jit(solution)/shard_map/all_to_all | solution.py:62
  122.7 48.8 %copy-start.11 = (f32[128,512]{1,0:T(8,128)}, f32[128,512]{1,0:T(8,128)S(1)}, u32[]{:S(2)}) copy-start(f32[128,512]{1,0:T(8,128)S(1)} %fusion.79) | copy-start | bytes 786436
  123.2 78.6 %copy-start.16 = (f32[128,256]{1,0:T(8,128)}, f32[128,256]{1,0:T(8,128)S(1)}, u32[]{:S(2)}) copy-start(f32[128,256]{1,0:T(8,128)S(1)} %fusion.42) | copy-start | bytes 393220
  123.6 0.6 copy-start.9
  201.8 4.9 copy-start.3
  201.8 6.5 %copy-start.24 = (f32[1024]{0:T(1024)S(1)}, f32[1024]{0:T(1024)}, u32[]{:S(2)}) copy-start(f32[1024]{0:T(1024)} %param.27) | copy-start | bytes 12292
  201.8 6.5 %copy-start.25 = (f32[128]{0:T(128)S(1)}, f32[128]{0:T(128)}, u32[]{:S(2)}) copy-start(f32[128]{0:T(128)} %param.20) | copy-start | bytes 1540
  208.3 1.0 copy-start.7
  209.2 0.6 copy-start.18
  250.2 48.8 %all-to-all-start.2 = ((bf16[128,97,128]{2,1,0:T(8,128)(2,1)}), bf16[128,97,128]{2,1,0:T(8,128)(2,1)}, u32[]{:S(2)}, u32[]{:S(2)}) async-start(bf16[128,97,128]{2,1,0:T(8,128)(2,1)} %reshape.180), calls=%async_computation.2 | async-start | bytes 6815744 | tf_op jit(solution)/shard_map/all_to_all | solution.py:87
  387.1 4.8 copy-start.10
  387.1 4.8 copy-start.17
  387.1 4.9 copy-start.19
  387.1 5.9 copy-start.14
  387.1 6.2 %copy-start.12 = (f32[128,512]{1,0:T(8,128)S(1)}, f32[128,512]{1,0:T(8,128)}, u32[]{:S(2)}) copy-start(f32[128,512]{1,0:T(8,128)} %copy-done.11) | copy-start | bytes 786436
  387.1 7.7 %copy-start.8 = (f32[128,1024]{1,0:T(8,128)S(1)}, f32[128,1024]{1,0:T(8,128)}, u32[]{:S(2)}) copy-start(f32[128,1024]{1,0:T(8,128)} %copy-done.7) | copy-start | bytes 1572868
  387.1 7.7 %copy-start.26 = (f32[128]{0:T(128)S(1)}, f32[128]{0:T(128)}, u32[]{:S(2)}) copy-start(f32[128]{0:T(128)} %param.20) | copy-start | bytes 1540
  387.1 128.2 %all-to-all-start.3 = ((f32[16,512,128]{2,1,0:T(8,128)}), f32[16,512,128]{2,1,0:T(8,128)}, u32[]{:S(2)}, u32[]{:S(2)}) async-start(f32[16,512,128]{2,1,0:T(8,128)} %bitcast.63), calls=%async_computation.3 | async-start | bytes 8388608 | tf_op jit(solution)/shard_map/all_to_all | solution.py:102
  391.8 4.8 copy-start.6
  391.9 188.7 %all-reduce.4.cloned.1.call-start = ((), (), s32[]{:S(2)}) async-start(), calls=%async_computation.4 | async-start | bytes 2686976 | tf_op jit(solution)/shard_map/psum | solution.py:77
  397.3 124.5 %copy-start.4 = (f32[512,256]{1,0:T(8,128)S(1)}, f32[512,256]{1,0:T(8,128)}, u32[]{:S(2)}) copy-start(f32[512,256]{1,0:T(8,128)} %param.22) | copy-start | bytes 1572868
  398.2 187.8 %copy-start.1 = (f32[164,1024]{1,0:T(8,128)S(1)}, f32[164,1024]{1,0:T(8,128)}, u32[]{:S(2)}) copy-start(f32[164,1024]{1,0:T(8,128)} %param.26) | copy-start | bytes 2015236
Sparse Core Ops, SparseCore 0:
  398.5 181.9 all-reduce.3
where the time goes:
time: 602 us; the launch traced here: 593 us
  local copies, waits for them, and re-layouts  154 us (26%)
  waiting for transfers between devices  141 us (23%)
  blocking collectives  138 us (23%)
  other arithmetic  105 us (17%)
  matrix products  24 us (4%)
  starting transfers between devices  15.9 us (3%)
  between operations  14.9 us (2%)
    psum x1, blocking collectives, body(): lax.psum((gradients[0], gradients[1], gradients[2], gradients[3], gradien...  117 us
    scatter-add x1, other arithmetic, body(): row_grad = jnp.zeros(table.shape, jnp.float32).at[served_ids.reshape(-1)]...  74.7 us
    psum x1, waiting for transfers between devices, body(): lax.psum((gradients[0], gradients[1], gradients[2], gradients[3], gradien...  57.9 us
    all_to_all x1, waiting for transfers between devices, body(): lax.all_to_all(send_grads.reshape(shards, capacity, feature_width), ('gro...  42 us
    all_to_all x1, waiting for transfers between devices, body(): lax.all_to_all(served_rows, ('group', 'member'), split_axis=0, concat_axi...  41.2 us
    gather x2, local copies, waits for them, and re-layouts, body(): served_rows = jnp.take(table, served_ids, axis=0).astype(jnp.bfloat16)  31.5 us
    scatter x1, local copies, waits for them, and re-layouts, body(): send_ids = jnp.zeros((shards * capacity,), jnp.int32).at[target].set(row_...  30.5 us
    gather x1, local copies, waits for them, and re-layouts, body(): gathered = fetched.reshape(shards * capacity, feature_width)[target]  30.3 us
  transfers between devices with their start and end apart: 4, of which 3 were waited for; matrix products, arithmetic and copies ran while one was open for 3% of the time, Pallas kernels for 0%

commit v1 on v0

v1 whole, which is shorter than its diff:
```python
import functools

import jax
import jax.numpy as jnp
import numpy as np
from jax import lax
from jax.experimental import pallas as pl
from jax.experimental.pallas import tpu as pltpu
from jax.sharding import PartitionSpec as P

embed_rate = 1.0

MESH = pl.DeviceIdType.MESH
N_DEV = 128
N_GROUP = 8
N_MEMBER = 16
E = 128
ROWS_DEV = 8192
NT = 8
HOT = 8
BAGS = 1024
MAIN = 96
GROUP = 8
PAIRS = [(i, j) for i in range(9) for j in range(i)]
BOT1, BOT2, TOPH, DENSE, TOPIN = 512, 256, 1024, 13, 164

TOP0_ROWS = 176
OFF_TOP0 = 0
OFF_BOT1 = 8 * TOP0_ROWS
OFF_BOT2 = OFF_BOT1 + 2 * BOT1
OFF_BOT0 = OFF_BOT2 + BOT2
OFF_TOP1 = OFF_BOT0 + 4 * 16
FLAT = 3072
PIECE = FLAT // N_GROUP
SMALL = PIECE // N_MEMBER

f32, bf16, i32 = jnp.float32, jnp.bfloat16, jnp.int32
VM = pltpu.VMEM


def iota(shape, dim):
    return lax.broadcasted_iota(i32, shape, dim)


def dot(a, b, dims):
    return lax.dot_general(a, b, (dims, ((), ())), preferred_element_type=f32)


NN = ((1,), (0,))
NT_ = ((1,), (1,))
TN = ((0,), (0,))


def halves(a):
    hi = a.astype(bf16)
    return hi, (a - hi.astype(f32)).astype(bf16)


def dot3(a, b, dims):
    return dot(a[0], b[0], dims) + (dot(a[0], b[1], dims) + dot(a[1], b[0], dims))


def coords():
    g, m = lax.axis_index("group"), lax.axis_index("member")
    return g // 2, g % 2, m // 4, m % 4


def peer(k):
    z, c, x, y = coords()
    kx = k % 4
    ky = (k // 4 + kx) % 4
    kz = (k // 16 + ky) % 4
    kc = k // 64
    return ((z + kz) % 4) * 2 + (c + kc) % 2, ((x + kx) % 4) * 4 + (y + ky) % 4


def origin(k):
    z, c, x, y = coords()
    kx = k % 4
    ky = (k // 4 + kx) % 4
    kz = (k // 16 + ky) % 4
    kc = k // 64
    return ((z + 4 - kz) % 4) * 2 + (c + 2 - kc) % 2, ((x + 4 - kx) % 4) * 4 + (y + 4 - ky) % 4


def sigmoid(v):
    return 1.0 / (1.0 + jnp.exp(-v))


def exchange_kernel(
    own_ref, row_ref, len_ref, x_ref, lg_ref, table_hbm, w0_ref, w1_ref, w2_ref, wt0_ref, wt1_ref,
    ids_out, gmain_out, gextra_out, flat_out,
    table_v, ids_send, ids_recv, ids_smem, stage, send_main, send_extra, recv_main, recv_extra,
    bag_of, bag_extra, st, pooled, pg, wt0_p, top_in, hid, dup,
    table_sem, smem_sem, ids_ssem, ids_rsem, row_ssem, row_esem, rowm_rsem, rowe_rsem,
    g_ssem, g_esem, gm_rsem, ge_rsem,
):
    g, m = lax.axis_index("group"), lax.axis_index("member")
    me = g * N_MEMBER + m

    table_copy = pltpu.make_async_copy(table_hbm, table_v, table_sem)
    table_copy.start()
    barrier = pltpu.get_barrier_semaphore()

    def greet(k, c):
        pl.semaphore_signal(barrier, 1, device_id=peer(k), device_id_type=MESH)
        return c

    lax.fori_loop(1, N_DEV, greet, 0)

    upper = (iota((256, 384), 0) < iota((256, 384), 1)).astype(bf16)
    dev_of = iota((128, 256), 0)
    lane = iota((1, 128), 1)

    def place(j, carry):
        count, acc = carry
        t = j // 4
        h = (2 * j) % 8
        length = len_ref[pl.ds(t, 1), :]
        own = jnp.concatenate([own_ref[pl.ds(2 * j, 1), :], own_ref[pl.ds(2 * j + 1, 1), :]], axis=1)
        row = jnp.concatenate([row_ref[pl.ds(2 * j, 1), :], row_ref[pl.ds(2 * j + 1, 1), :]], axis=1)
        own = jnp.where(jnp.concatenate([h < length, h + 1 < length], axis=1), own, -1)
        hit = own == dev_of
        hit_f = hit.astype(f32)
        hit_b = hit_f.astype(bf16)
        ranks = dot(hit_b, upper, NN)
        before = ranks[:, 0:256] + jnp.concatenate([count, count], axis=1)
        pos = jnp.sum(before * hit_f, axis=0, keepdims=True).astype(i32)
        at = (pos == dev_of).astype(f32)
        bag_lo = jnp.concatenate([lane, lane], axis=1).astype(f32)
        vals = jnp.concatenate(
            [
                at * (row // 128).astype(f32),
                at * (row % 128).astype(f32),
                at * (t + 1).astype(f32),
                at * bag_lo,
            ],
            axis=0,
        ).astype(bf16)
        return count + ranks[:, 256:384], acc + dot(vals, hit_b, NT_)

    count, acc = lax.fori_loop(
        0, 32, place, (jnp.zeros((128, 128), f32), jnp.zeros((512, 128), f32)), unroll=2
    )
    ids = (acc[0:128] * 128.0 + acc[128:256]).T
    ids = jnp.where(iota((128, 128), 1) == 127, count, ids).astype(i32)
    for d in range(N_DEV):
        ids_send[d] = ids[d : d + 1, :]
    bag = acc[256:384] * 128.0 + acc[384:512] - 128.0
    pl.semaphore_wait(barrier, N_DEV - 1)

    def ids_copy(k):
        to_g, to_m = peer(k)
        return pltpu.make_async_remote_copy(
            ids_send.at[to_g * N_MEMBER + to_m], ids_recv.at[me], ids_ssem, ids_rsem,
            device_id=(to_g, to_m), device_id_type=MESH,
        )

    def send_ids(k, c):
        ids_copy(k).start()
        return c

    lax.fori_loop(1, N_DEV, send_ids, 0)
    ids_recv[me] = ids_send[me]

    bag_i = bag.astype(i32)
    for d in range(N_DEV):
        bag_of[d] = jnp.broadcast_to(bag_i[0:MAIN, d : d + 1], (MAIN, 128))
    bag_t = bag.T.astype(i32)
    bag_extra[...] = jnp.broadcast_to(bag_t[:, MAIN : MAIN + 1], (128, 128))
    wait_ids = pltpu.make_async_copy(ids_send.at[pl.ds(0, 127)], ids_recv.at[pl.ds(0, 127)], ids_rsem)
    wait_ids.wait()
    ids_recv[...] = jnp.clip(ids_recv[...], 0, ROWS_DEV - 1)
    smem_copy = pltpu.make_async_copy(ids_recv, ids_smem, smem_sem)
    smem_copy.start()
    smem_copy.wait()
    table_copy.wait()

    def gather(d, slot):
        for i in range(MAIN):
            stage[i : i + 1, :] = table_v[pl.ds(ids_smem[d, 0, i] & (ROWS_DEV - 1), 1), :]
        send_main[slot] = stage[...].astype(bf16)
        send_extra[slot] = table_v[pl.ds(ids_smem[d, 0, MAIN] & (ROWS_DEV - 1), 1), :]

    def rows_copies(k):
        to = peer(k)
        return (
            pltpu.make_async_remote_copy(
                send_main.at[k], recv_main.at[k], row_ssem, rowm_rsem.at[k // GROUP],
                device_id=to, device_id_type=MESH,
            ),
            pltpu.make_async_remote_copy(
                send_extra.at[k], recv_extra.at[k], row_esem, rowe_rsem,
                device_id=to, device_id_type=MESH,
            ),
        )

    def serve(k, c):
        to_g, to_m = peer(k)
        gather(to_g * N_MEMBER + to_m, k)
        for copy in rows_copies(k):
            copy.start()
        return c

    lax.fori_loop(1, N_DEV, serve, 0)
    gather(me, 0)
    recv_main[0] = send_main[0]
    recv_extra[0] = send_extra[0]

    top_in[...] = jnp.zeros_like(top_in)
    top_in[0:DENSE, :] = x_ref[...]
    x_pad = top_in[0:128, :]
    x_h = halves(x_pad)
    w0_t = jnp.concatenate([w0_ref[...], jnp.zeros((128 - DENSE, BOT1), f32)], axis=0).T
    w0_th = halves(w0_t)
    h1p = dot3(w0_th, x_h, NN)
    s1 = sigmoid(h1p)
    h1_h = halves(h1p * s1)
    d1 = s1 * (1.0 + h1p * (1.0 - s1))
    w1_h = halves(w1_ref[...])
    w1_th = halves(w1_ref[...].T)
    h2p = dot3(w1_th, h1_h, NN)
    s2 = sigmoid(h2p)
    h2_h = halves(h2p * s2)
    d2 = s2 * (1.0 + h2p * (1.0 - s2))
    w2_h = halves(w2_ref[...])
    w2_th = halves(w2_ref[...].T)
    bp = dot3(w2_th, h2_h, NN)
    s3 = sigmoid(bp)
    bottom = bp * s3
    d3 = s3 * (1.0 + bp * (1.0 - s3))
    top_in[0:128, :] = bottom
    wt0_p[...] = jnp.zeros_like(wt0_p)
    wt0_p[0:TOPIN, :] = wt0_ref[...]
    wt0_h = halves(wt0_p[...])
    wt0_th = halves(wt0_p[...].T)

    def one_hot(bags):
        return jnp.concatenate(
            [(bags == iota((1, 128), 1) + 128 * t).astype(f32).astype(bf16) for t in range(NT)], axis=1
        )

    def pool_main(q):
        for i in range(GROUP):
            from_g, from_m = origin(q * GROUP + i)
            st[pl.ds(i * MAIN, MAIN), :] = one_hot(bag_of[from_g * N_MEMBER + from_m])
        rows = recv_main[pl.ds(q * GROUP, GROUP)].reshape(GROUP * MAIN, E)
        pooled[...] += dot(rows, st[...], TN)

    def wait_rows(q, count):
        pltpu.make_async_copy(
            send_main.at[pl.ds(0, count)], recv_main.at[pl.ds(0, count)], rowm_rsem.at[q]
        ).wait()

    pooled[...] = jnp.zeros_like(pooled)
    wait_rows(0, GROUP - 1)
    pool_main(0)

    def pool_step(q, c):
        wait_rows(q, GROUP)
        pool_main(q)
        return c

    lax.fori_loop(1, N_DEV // GROUP, pool_step, 0)
    pltpu.make_async_copy(
        send_extra.at[pl.ds(0, 127)], recv_extra.at[pl.ds(0, 127)], rowe_rsem
    ).wait()
    for k in range(N_DEV):
        from_g, from_m = origin(k)
        hid[pl.ds(from_g * N_MEMBER + from_m, 1), :] = recv_extra[k]
    pooled[...] += dot(hid[0:128, :].astype(bf16), one_hot(bag_extra[...]), TN)

    z = [bottom] + [pooled[:, 128 * t : 128 * (t + 1)] for t in range(NT)]
    for n, (i, j) in enumerate(PAIRS):
        top_in[128 + n : 129 + n, :] = jnp.sum(z[i] * z[j], axis=0, keepdims=True)
    top_h = halves(top_in[...])
    up = dot3(wt0_th, top_h, NN)
    su = sigmoid(up)
    hid[...] = up * su
    lg = lg_ref[...]
    wt1_col = jnp.broadcast_to(wt1_ref[...], (128, TOPH)).T
    dup[...] = wt1_col * lg * (su * (1.0 + up * (1.0 - su)))
    dup_h = halves(dup[...])
    d_top = dot3(wt0_h, dup_h, NN)
    d_pair = {}
    for n, (i, j) in enumerate(PAIRS):
        d_pair[i, j] = d_pair[j, i] = d_top[128 + n : 129 + n, :]
    d_z = []
    for i in range(9):
        total = None
        for j in range(9):
            if j != i:
                term = d_pair[i, j] * z[j]
                total = term if total is None else total + term
        d_z.append(total)
        if i > 0:
            pg[128 * (i - 1) : 128 * i, :] = total.T.astype(bf16)

    pltpu.make_async_copy(send_main.at[pl.ds(0, 127)], recv_main.at[pl.ds(0, 127)], row_ssem).wait()
    pltpu.make_async_copy(send_extra.at[pl.ds(0, 127)], recv_extra.at[pl.ds(0, 127)], row_esem).wait()

    extra = dot(one_hot(bag_extra[...]), pg[...], NN)
    for d in range(N_DEV):
        send_extra[d] = extra[d : d + 1, :]

    def grad_copies(k):
        to_g, to_m = peer(k)
        return (
            pltpu.make_async_remote_copy(
                send_main.at[k], gmain_out.at[me], g_ssem, gm_rsem,
                device_id=(to_g, to_m), device_id_type=MESH,
            ),
            pltpu.make_async_remote_copy(
                send_extra.at[to_g * N_MEMBER + to_m], gextra_out.at[me], g_esem, ge_rsem,
                device_id=(to_g, to_m), device_id_type=MESH,
            ),
        )

    def expand(q):
        for i in range(GROUP):
            to_g, to_m = peer(q * GROUP + i)
            st[pl.ds(i * MAIN, MAIN), :] = one_hot(bag_of[to_g * N_MEMBER + to_m])
        grads = dot(st[...], pg[...], NN).astype(bf16)
        send_main[pl.ds(q * GROUP, GROUP)] = grads.reshape(GROUP, MAIN, E)

    def start_grads(k, c):
        for copy in grad_copies(k):
            copy.start()
        return c

    expand(0)
    lax.fori_loop(1, GROUP, start_grads, 0)

    def expand_step(q, c):
        expand(q)
        lax.fori_loop(q * GROUP, q * GROUP + GROUP, start_grads, 0)
        return c

    lax.fori_loop(1, N_DEV // GROUP, expand_step, 0)
    gmain_out[me] = send_main[0]
    gextra_out[me] = send_extra[me]
    ids_out[...] = ids_recv[...]

    flat_out[...] = jnp.zeros_like(flat_out)
    g_t0 = dot3(top_h, dup_h, NT_).astype(bf16)
    for c in range(8):
        flat_out[OFF_TOP0 + c * TOP0_ROWS : OFF_TOP0 + (c + 1) * TOP0_ROWS, :] = g_t0[
            0:TOP0_ROWS, 128 * c : 128 * (c + 1)
        ]
    lg_h = halves(jnp.broadcast_to(lg, (8, 128)))
    g_t1 = dot3(lg_h, halves(hid[...]), NT_)[0:1]
    g_t1 = jnp.concatenate([g_t1[:, 128 * c : 128 * (c + 1)] for c in range(8)], axis=0)
    flat_out[OFF_TOP1 : OFF_TOP1 + 16, :] = jnp.concatenate([g_t1, g_t1], axis=0).astype(bf16)
    d_bp = halves((d_top[0:128] + d_z[0]) * d3)
    flat_out[OFF_BOT2 : OFF_BOT2 + BOT2, :] = dot3(h2_h, d_bp, NT_).astype(bf16)
    d_h2p = halves(dot3(w2_h, d_bp, NN) * d2)
    g_b1 = dot3(h1_h, d_h2p, NT_).astype(bf16)
    for c in range(2):
        flat_out[OFF_BOT1 + c * BOT1 : OFF_BOT1 + (c + 1) * BOT1, :] = g_b1[:, 128 * c : 128 * (c + 1)]
    d_h1p = halves(dot3(w1_h, d_h2p, NN) * d1)
    g_b0 = dot3(x_h, d_h1p, NT_)[0:16].astype(bf16)
    for c in range(4):
        flat_out[OFF_BOT0 + c * 16 : OFF_BOT0 + (c + 1) * 16, :] = g_b0[:, 128 * c : 128 * (c + 1)]

    pltpu.make_async_copy(ids_send.at[pl.ds(0, 127)], ids_recv.at[pl.ds(0, 127)], ids_ssem).wait()
    pltpu.make_async_copy(send_main.at[pl.ds(0, 127)], recv_main.at[pl.ds(0, 127)], g_ssem).wait()
    pltpu.make_async_copy(send_extra.at[pl.ds(0, 127)], recv_extra.at[pl.ds(0, 127)], g_esem).wait()
    pltpu.make_async_copy(send_main.at[pl.ds(0, 127)], gmain_out.at[pl.ds(0, 127)], gm_rsem).wait()
    pltpu.make_async_copy(send_extra.at[pl.ds(0, 127)], gextra_out.at[pl.ds(0, 127)], ge_rsem).wait()


WAYS = 4


def scatter_kernel(ids_ref, gmain_ref, gextra_ref, table_ref, new_ref, change_ref, sums, stage):
    sums[...] = jnp.zeros_like(sums)

    def source(s, c):
        stage[0:MAIN, :] = gmain_ref[s].astype(f32)
        stage[MAIN : MAIN + 1, :] = gextra_ref[s]
        count = ids_ref[s, 0, 127]

        def batch(b, c):
            first = b * 8
            for half in range(0, 8, WAYS):
                rows, total = [], []
                for i in range(WAYS):
                    r = ids_ref[s, 0, first + half + i]
                    rows.append(r)
                    total.append(
                        sums[i, pl.ds(r, 1), :] + stage[pl.ds(first + half + i, 1), :]
                    )
                for i in range(WAYS):
                    sums[i, pl.ds(rows[i], 1), :] = total[i]
            return c

        lax.fori_loop(0, (count + 7) // 8, batch, 0)
        return c

    stage[...] = jnp.zeros_like(stage)
    lax.fori_loop(0, N_DEV, source, 0)

    def finish(b, c):
        at = pl.ds(pl.multiple_of(b * 256, 256), 256)
        total = sums[0, at, :]
        for i in range(1, WAYS):
            total = total + sums[i, at, :]
        total = -embed_rate * total
        new_ref[at, :] = table_ref[at, :] + total
        change_ref[at, :] = total.astype(bf16)
        return c

    lax.fori_loop(0, ROWS_DEV // 256, finish, 0)


def member_peer(k, sign):
    x, y = lax.axis_index("member") // 4, lax.axis_index("member") % 4
    kx = k % 4
    ky = (k // 4 + kx) % 4
    if sign < 0:
        kx, ky = (4 - kx) % 4, (4 - ky) % 4
    return ((x + kx) % 4) * 4 + (y + ky) % 4


def parity_kernel(
    change_ref, parity_ref, flat_ref,
    new_ref, g0_ref, g1_ref, g2_ref, gt0_ref, gt1_ref,
    pieces, part_z, sum_z, part_xy, sum_xy, all_xy, all_z_send, all_z,
    ch_ssem, ch_rsem, rz_ssem, rz_rsem, rx_ssem, rx_rsem, ax_ssem, ax_rsem, az_ssem, az_rsem,
):
    g, m = lax.axis_index("group"), lax.axis_index("member")
    barrier = pltpu.get_barrier_semaphore()
    for j in range(1, N_GROUP):
        pl.semaphore_signal(barrier, 1, device_id=((g + j) % N_GROUP, m), device_id_type=MESH)
    for k in range(1, N_MEMBER):
        pl.semaphore_signal(barrier, 1, device_id=(g, member_peer(k, 1)), device_id_type=MESH)
    pl.semaphore_wait(barrier, N_GROUP - 1 + N_MEMBER - 1)

    def remote(src, dst, ssem, rsem, to):
        return pltpu.make_async_remote_copy(src, dst, ssem, rsem, device_id=to, device_id_type=MESH)

    rows = ROWS_DEV // N_MEMBER

    def change_copy(k):
        to = member_peer(k, 1)
        return remote(
            change_ref.at[pl.ds(pl.multiple_of(to * rows, rows), rows)], pieces.at[k], ch_ssem.at[k], ch_rsem.at[k],
            (g, to),
        )

    def rz_copy(j):
        to = (g + j) % N_GROUP
        return remote(
            flat_ref.at[pl.ds(pl.multiple_of(to * PIECE, PIECE), PIECE)], part_z.at[j], rz_ssem.at[j], rz_rsem.at[j],
            (to, m),
        )

    def rx_copy(k):
        to = member_peer(k, 1)
        return remote(
            sum_z.at[pl.ds(pl.multiple_of(to * SMALL, SMALL), SMALL)], part_xy.at[k], rx_ssem.at[k], rx_rsem.at[k],
            (g, to),
        )

    def ax_copy(k):
        return remote(sum_xy, all_xy.at[m], ax_ssem.at[k], ax_rsem.at[k], (g, member_peer(k, 1)))

    def az_copy(j):
        return remote(all_z_send, all_z.at[g], az_ssem.at[j], az_rsem.at[j], ((g + j) % N_GROUP, m))

    for j in range(1, N_GROUP):
        rz_copy(j).start()
    for k in range(1, 6):
        change_copy(k).start()
    total = flat_ref[pl.ds(pl.multiple_of(g * PIECE, PIECE), PIECE), :].astype(f32)
    for j in range(1, N_GROUP):
        rz_copy(j).wait()
        total = total + part_z[j].astype(f32)
    sum_z[...] = total
    for k in range(1, N_MEMBER):
        rx_copy(k).start()
    for k in range(6, 11):
        change_copy(k).start()
    total = sum_z[pl.ds(pl.multiple_of(m * SMALL, SMALL), SMALL), :]
    for k in range(1, N_MEMBER):
        rx_copy(k).wait()
        total = total + part_xy[k]
    sum_xy[...] = total
    for k in range(1, N_MEMBER):
        ax_copy(k).start()
    for k in range(11, N_MEMBER):
        change_copy(k).start()
    all_xy[m] = total
    for k in range(1, N_MEMBER):
        ax_copy(k).wait()
    all_z_send[...] = all_xy[...].reshape(PIECE, E).astype(bf16)
    for j in range(1, N_GROUP):
        az_copy(j).start()

    def weights(k):
        source = member_peer(k, -1).astype(f32) / N_MEMBER
        one = jnp.ones((1, 128), f32)
        return 1.0 / (one + source), 1.0 / (one * 2.0 + source)

    for k in range(1, N_MEMBER):
        change_copy(k).wait()
    coef = [weights(k) for k in range(N_MEMBER)]
    own_at = m * rows

    def combine(b, c):
        at = pl.ds(pl.multiple_of(b * 32, 32), 32)
        part = change_ref[pl.ds(pl.multiple_of(own_at + b * 32, 32), 32), :].astype(f32)
        first, second = coef[0][0] * part, coef[0][1] * part
        for k in range(1, N_MEMBER):
            part = pieces[k, at, :].astype(f32)
            first = first + coef[k][0] * part
            second = second + coef[k][1] * part
        new_ref[at, 0:128] = parity_ref[at, 0:128] + first
        new_ref[at, 128:256] = parity_ref[at, 128:256] + second
        return c

    lax.fori_loop(0, rows // 32, combine, 0)

    all_z[g] = all_z_send[...]
    for j in range(1, N_GROUP):
        az_copy(j).wait()
    for c in range(8):
        gt0_ref[:, 128 * c : 128 * (c + 1)] = piece_rows(all_z, OFF_TOP0 + c * TOP0_ROWS, TOP0_ROWS)[0:TOPIN]
    for c in range(2):
        g1_ref[:, 128 * c : 128 * (c + 1)] = piece_rows(all_z, OFF_BOT1 + c * BOT1, BOT1)
    g2_ref[...] = piece_rows(all_z, OFF_BOT2, BOT2)
    for c in range(4):
        g0_ref[:, 128 * c : 128 * (c + 1)] = piece_rows(all_z, OFF_BOT0 + c * 16, 16)[0:DENSE]
    top1 = piece_rows(all_z, OFF_TOP1, 16)
    for c in range(8):
        gt1_ref[:, 128 * c : 128 * (c + 1)] = top1[c : c + 1, :]


def piece_rows(ref, start, count):
    out = []
    while count > 0:
        p, at = start // PIECE, start % PIECE
        n = min(count, PIECE - at)
        out.append(ref[p, at : at + n, :].astype(f32))
        start, count = start + n, count - n
    return out[0] if len(out) == 1 else jnp.concatenate(out, axis=0)


def body(
    dense_in, lookup_owner, lookup_row, bag_length, logit_grad, table, parity,
    w_bottom0, w_bottom1, w_bottom2, w_top0, w_top1,
):
    owner = lookup_owner.transpose(1, 2, 0).reshape(NT * HOT, 128)
    row = lookup_row.transpose(1, 2, 0).reshape(NT * HOT, 128)
    vmem = pl.BlockSpec(memory_space=VM)
    anyw = pl.BlockSpec(memory_space=pl.ANY)
    smem = pl.BlockSpec(memory_space=pltpu.SMEM)
    dma = pltpu.SemaphoreType.DMA
    sds = jax.ShapeDtypeStruct
    ids, gmain, gextra, flat = pl.pallas_call(
        exchange_kernel,
        out_shape=(
            sds((N_DEV, 1, 128), i32),
            sds((N_DEV, MAIN, E), bf16),
            sds((N_DEV, 1, E), f32),
            sds((FLAT, E), bf16),
        ),
        in_specs=[vmem] * 5 + [anyw] + [vmem] * 5,
        out_specs=(vmem,) * 4,
        scratch_shapes=[
            VM((ROWS_DEV, E), f32),
            VM((N_DEV, 1, 128), i32),
            VM((N_DEV, 1, 128), i32),
            pltpu.SMEM((N_DEV, 1, 128), i32),
            VM((MAIN, E), f32),
            VM((N_DEV, MAIN, E), bf16),
            VM((N_DEV, 1, E), f32),
            VM((N_DEV, MAIN, E), bf16),
            VM((N_DEV, 1, E), f32),
            VM((N_DEV, MAIN, 128), i32),
            VM((128, 128), i32),
            VM((GROUP * MAIN, BAGS), bf16),
            VM((E, BAGS), f32),
            VM((BAGS, E), bf16),
            VM((256, TOPH), f32),
            VM((256, 128), f32),
            VM((TOPH, 128), f32),
            VM((TOPH, 128), f32),
            dma, dma, dma, dma, dma, dma, dma((N_DEV // GROUP,)), dma, dma, dma, dma, dma,
        ],
        compiler_params=pltpu.CompilerParams(
            collective_id=0, has_side_effects=True, vmem_limit_bytes=56 << 20
        ),
    )(
        owner, row, bag_length.T, dense_in.T, logit_grad.reshape(1, 128), table,
        w_bottom0, w_bottom1, w_bottom2, w_top0, w_top1.reshape(1, TOPH),
    )
    new_table, change = pl.pallas_call(
        scatter_kernel,
        out_shape=(sds((ROWS_DEV, E), f32), sds((ROWS_DEV, E), bf16)),
        in_specs=[smem, vmem, vmem, vmem],
        out_specs=(vmem, vmem),
        scratch_shapes=[VM((WAYS, ROWS_DEV, E), f32), VM((MAIN + 8, E), f32)],
        compiler_params=pltpu.CompilerParams(vmem_limit_bytes=56 << 20),
    )(ids, gmain, gextra, table)
    new_parity, g0, g1, g2, gt0, gt1 = pl.pallas_call(
        parity_kernel,
        out_shape=(
            sds(parity.shape, f32),
            sds((DENSE, BOT1), f32),
            sds((BOT1, BOT2), f32),
            sds((BOT2, E), f32),
            sds((TOPIN, TOPH), f32),
            sds((1, TOPH), f32),
        ),
        in_specs=[vmem] * 3,
        out_specs=(vmem,) * 6,
        scratch_shapes=[
            VM((N_MEMBER, ROWS_DEV // N_MEMBER, E), bf16),
            VM((N_GROUP, PIECE, E), bf16),
            VM((PIECE, E), f32),
            VM((N_MEMBER, SMALL, E), f32),
            VM((SMALL, E), f32),
            VM((N_MEMBER, SMALL, E), f32),
            VM((PIECE, E), bf16),
            VM((N_GROUP, PIECE, E), bf16),
            dma((N_MEMBER,)), dma((N_MEMBER,)), dma((N_GROUP,)), dma((N_GROUP,)),
            dma((N_MEMBER,)), dma((N_MEMBER,)), dma((N_MEMBER,)), dma((N_MEMBER,)),
            dma((N_GROUP,)), dma((N_GROUP,)),
        ],
        compiler_params=pltpu.CompilerParams(
            collective_id=1, has_side_effects=True, vmem_limit_bytes=56 << 20
        ),
    )(change, parity, flat)
    return new_table, new_parity, g0, g1, g2, gt0, gt1.reshape(TOPH)


def solution(mesh):
    rows = P(("group", "member"), None)
    cube = P(("group", "member"), None, None)
    in_specs = (rows, cube, cube, rows, P(("group", "member")), rows, rows, P(), P(), P(), P(), P())
    out_specs = (rows, rows, P(), P(), P(), P(), P())
    return jax.shard_map(body, mesh=mesh, in_specs=in_specs, out_specs=out_specs, check_vma=False)
```

time: 602 us -> 210 us (0.35); the launches traced: 593 us -> 209 us
  Pallas kernels: 0 us -> 199 us
  local copies, waits for them, and re-layouts: 154 us -> 9.97 us
  waiting for transfers between devices: 141 us -> 0 us
  blocking collectives: 138 us -> 0 us
  other arithmetic: 105 us -> 0 us
  matrix products: 24 us -> 0 us
  starting transfers between devices: 15.9 us -> 0 us
  between operations: 14.9 us -> 0.66 us
    pallas_call x0 -> x3, Pallas kernels: none -> 199 us  [the longest x1 122 us: body(): pl.pallas_call(exchange_kernel, out_shape=(sds((N_DEV, 1, 128), i32), sds...]
    psum x1 -> x0, blocking collectives: 117 us -> none  [body(): lax.psum((gradients[0], gradients[1], gradients[2], gradients[3], gradien...]
    all_to_all x3 -> x0, waiting for transfers between devices: 83.1 us -> none  [the longest x1 42 us: body(): lax.all_to_all(send_grads.reshape(shards, capacity, feature_width), ('gro...]
    scatter-add x2 -> x0, other arithmetic: 78.3 us -> none  [the longest x1 74.7 us: body(): row_grad = jnp.zeros(table.shape, jnp.float32).at[served_ids.reshape(-1)]...]
    gather x4 -> x0, local copies, waits for them, and re-layouts: 62.7 us -> none  [the longest x2 31.5 us: body(): served_rows = jnp.take(table, served_ids, axis=0).astype(jnp.bfloat16)]
    psum x1 -> x0, waiting for transfers between devices: 57.9 us -> none  [body(): lax.psum((gradients[0], gradients[1], gradients[2], gradients[3], gradien...]
    scatter x2 -> x0, local copies, waits for them, and re-layouts: 53.8 us -> none  [the longest x1 30.5 us: body(): send_ids = jnp.zeros((shards * capacity,), jnp.int32).at[target].set(row_...]
    dot_general x17 -> x0, matrix products: 24 us -> none  [the longest x1 6.44 us: body(): jnp.einsum('mre,km->rke', pieces, coeffs, precision=lax.Precision.HIGHEST)]
  transfers between devices with their start and end apart: 4 -> 0, of which waited for: 3 -> 0; matrix products, arithmetic and copies ran while one was open for 3% -> 0% of each run, Pallas kernels for 0% -> 0%
where the time goes in v1:
time: 210 us; the launch traced here: 209 us
  Pallas kernels  199 us (95%)
  local copies, waits for them, and re-layouts  9.97 us (5%)
    pallas_call x1, Pallas kernels, body(): pl.pallas_call(exchange_kernel, out_shape=(sds((N_DEV, 1, 128), i32), sds...  122 us
    pallas_call x1, Pallas kernels, body(): pl.pallas_call(parity_kernel, out_shape=(sds(parity.shape, f32), sds((DEN...  51.5 us
    pallas_call x1, Pallas kernels, body(): pl.pallas_call(scatter_kernel, out_shape=(sds((ROWS_DEV, E), f32), sds((R...  25 us
    unnamed x6, local copies, waits for them, and re-layouts  9.97 us

profile of v1, /device:TPU:1, one launch (start us, length us, event | category | flops | bytes accessed | tf_op | source)
XLA Modules:
  0.0 209.3 jit_solution(5502305415599914504)
XLA Ops:
  0.6 122.2 %shard_map.171 = (s32[128,1,128]{2,1,0:T(1,128)}, bf16[128,96,128]{2,1,0:T(8,128)(2,1)}, f32[128,1,128]{2,1,0:T(1,128)}, bf16[3072,128]{1,0:T(8,128)(2,1)}) custom-call(s32[64,128]{1,0:T(8,128)} %bitcast.11, s32[64,128]{1,0:T(8,128)} %bitcast.12, s32[8,128]{1,0:T(8,128)} %bitcast.15, f32[13,128]{1,0:T(8,128)} %bitcast.13, f32[1,128]{1,0:T(1,128)} %bitcast.17, ...), custom_call_target="tpu_custom_call" | custom-call | tf_op jit(solution)/shard_map/pallas_call | solution.py:560
  122.8 25.0 %shard_map.172 = (f32[8192,128]{1,0:T(8,128)}, bf16[8192,128]{1,0:T(8,128)(2,1)}) custom-call(s32[128,1,128]{2,1,0:T(1,128)} %get-tuple-element.19.ids_ref, bf16[128,96,128]{2,1,0:T(8,128)(2,1)} %get-tuple-element.20.gmain_ref, f32[128,1,128]{2,1,0:T(1,128)} %get-tuple-element.21.gextra_ref, f32[8192,128]{1,0:T(8,128)} %table_ref.1), custom_call_target="tpu_custom_call" | custom-call | tf_op jit(solution)/shard_map/pallas_call | solution.py:598
  147.8 51.5 %shard_map.173 = (f32[512,256]{1,0:T(8,128)}, f32[13,512]{1,0:T(8,128)}, f32[512,256]{1,0:T(8,128)}, f32[256,128]{1,0:T(8,128)}, f32[164,1024]{1,0:T(8,128)}, /*index=5*/f32[1,1024]{1,0:T(1,128)}) custom-call(bf16[8192,128]{1,0:T(8,128)(2,1)} %get-tuple-element.23.change_ref, f32[512,256]{1,0:T(8,128)} %parity_ref.1, ...), custom_call_target="tpu_custom_call" | custom-call | tf_op jit(solution)/shard_map/pallas_call | solution.py:606
  199.3 1.9 copy.25
  201.2 1.4 copy.26
  202.6 1.9 copy.27
  204.4 1.6 copy.28
  206.0 2.0 copy.29
  208.0 1.3 copy.30

commit v2 on v1

--- a/solution.py
+++ b/solution.py
@@ -20,6 +20,7 @@
 HOT = 8
 BAGS = 1024
 MAIN = 96
+SERVE = 16
 GROUP = 8
 PAIRS = [(i, j) for i in range(9) for j in range(i)]
 BOT1, BOT2, TOPH, DENSE, TOPIN = 512, 256, 1024, 13, 164
@@ -31,6 +32,7 @@
 OFF_BOT0 = OFF_BOT2 + BOT2
 OFF_TOP1 = OFF_BOT0 + 4 * 16
 FLAT = 3072
+HALF = FLAT // 2
 PIECE = FLAT // N_GROUP
 SMALL = PIECE // N_MEMBER
 
@@ -83,6 +85,24 @@
     return ((z + 4 - kz) % 4) * 2 + (c + 2 - kc) % 2, ((x + 4 - kx) % 4) * 4 + (y + 4 - ky) % 4
 
 
+def each_peer(act):
+    z, c, x, y = coords()
+    member = [((x + r % 4) % 4) * 4 + (y + (r // 4 + r % 4) % 4) % 4 for r in range(16)]
+
+    def sixteen(a, first):
+        group = [((z + a + ky) % 4) * 2 + (c + a // 4) % 2 for ky in range(4)]
+        for r in range(first, 16):
+            act(a * 16 + r, (group[(r // 4 + r % 4) % 4], member[r]))
+
+    sixteen(0, 1)
+
+    def loop(a, carry):
+        sixteen(a, 0)
+        return carry
+
+    lax.fori_loop(1, 8, loop, 0)
+
+
 def sigmoid(v):
     return 1.0 / (1.0 + jnp.exp(-v))
 
@@ -91,9 +111,9 @@
     own_ref, row_ref, len_ref, x_ref, lg_ref, table_hbm, w0_ref, w1_ref, w2_ref, wt0_ref, wt1_ref,
     ids_out, gmain_out, gextra_out, flat_out,
     table_v, ids_send, ids_recv, ids_smem, stage, send_main, send_extra, recv_main, recv_extra,
-    bag_of, bag_extra, st, pooled, pg, wt0_p, top_in, hid, dup,
+    hits, vals, bag_of, bag_extra, st, pooled, pg, wt0_p, top_in, hid, dup,
     table_sem, smem_sem, ids_ssem, ids_rsem, row_ssem, row_esem, rowm_rsem, rowe_rsem,
-    g_ssem, g_esem, gm_rsem, ge_rsem,
+    g_ssem, g_esem, gm_rsem, ge_rsem, flat, flat_half, own_sem, half_ssem, half_rsem,
 ):
     g, m = lax.axis_index("group"), lax.axis_index("member")
     me = g * N_MEMBER + m
@@ -102,46 +122,37 @@
     table_copy.start()
     barrier = pltpu.get_barrier_semaphore()
 
-    def greet(k, c):
-        pl.semaphore_signal(barrier, 1, device_id=peer(k), device_id_type=MESH)
-        return c
-
-    lax.fori_loop(1, N_DEV, greet, 0)
+    each_peer(lambda k, to: pl.semaphore_signal(barrier, 1, device_id=to, device_id_type=MESH))
 
     upper = (iota((256, 384), 0) < iota((256, 384), 1)).astype(bf16)
     dev_of = iota((128, 256), 0)
     lane = iota((1, 128), 1)
-
-    def place(j, carry):
-        count, acc = carry
+    bag_lo = jnp.concatenate([lane, lane], axis=1).astype(f32).astype(bf16)
+
+    def place(j, count):
         t = j // 4
         h = (2 * j) % 8
         length = len_ref[pl.ds(t, 1), :]
         own = jnp.concatenate([own_ref[pl.ds(2 * j, 1), :], own_ref[pl.ds(2 * j + 1, 1), :]], axis=1)
         row = jnp.concatenate([row_ref[pl.ds(2 * j, 1), :], row_ref[pl.ds(2 * j + 1, 1), :]], axis=1)
         own = jnp.where(jnp.concatenate([h < length, h + 1 < length], axis=1), own, -1)
-        hit = own == dev_of
-        hit_f = hit.astype(f32)
-        hit_b = hit_f.astype(bf16)
+        hit = (own == dev_of).astype(f32)
+        hit_b = hit.astype(bf16)
         ranks = dot(hit_b, upper, NN)
         before = ranks[:, 0:256] + jnp.concatenate([count, count], axis=1)
-        pos = jnp.sum(before * hit_f, axis=0, keepdims=True).astype(i32)
-        at = (pos == dev_of).astype(f32)
-        bag_lo = jnp.concatenate([lane, lane], axis=1).astype(f32)
-        vals = jnp.concatenate(
-            [
-                at * (row // 128).astype(f32),
-                at * (row % 128).astype(f32),
-                at * (t + 1).astype(f32),
-                at * bag_lo,
-            ],
-            axis=0,
-        ).astype(bf16)
-        return count + ranks[:, 256:384], acc + dot(vals, hit_b, NT_)
-
-    count, acc = lax.fori_loop(
-        0, 32, place, (jnp.zeros((128, 128), f32), jnp.zeros((512, 128), f32)), unroll=2
-    )
+        pos = jnp.sum(before * hit, axis=0, keepdims=True).astype(i32)
+        at = (pos == dev_of).astype(f32).astype(bf16)
+        hits[j] = hit_b
+        vals[j, 0:128, :] = at * (row // 128).astype(f32).astype(bf16)
+        vals[j, 128:256, :] = at * (row % 128).astype(f32).astype(bf16)
+        vals[j, 256:384, :] = at * (t + 1).astype(f32).astype(bf16)
+        vals[j, 384:512, :] = at * bag_lo
+        return count + ranks[:, 256:384]
+
+    count = lax.fori_loop(0, 32, place, jnp.zeros((128, 128), f32), unroll=4)
+    acc = dot(vals[0], hits[0], NT_)
+    for j in range(1, 32):
+        acc = acc + dot(vals[j], hits[j], NT_)
     ids = (acc[0:128] * 128.0 + acc[128:256]).T
     ids = jnp.where(iota((128, 128), 1) == 127, count, ids).astype(i32)
     for d in range(N_DEV):
@@ -149,41 +160,38 @@
     bag = acc[256:384] * 128.0 + acc[384:512] - 128.0
     pl.semaphore_wait(barrier, N_DEV - 1)
 
-    def ids_copy(k):
-        to_g, to_m = peer(k)
-        return pltpu.make_async_remote_copy(
-            ids_send.at[to_g * N_MEMBER + to_m], ids_recv.at[me], ids_ssem, ids_rsem,
-            device_id=(to_g, to_m), device_id_type=MESH,
-        )
-
-    def send_ids(k, c):
-        ids_copy(k).start()
-        return c
-
-    lax.fori_loop(1, N_DEV, send_ids, 0)
-    ids_recv[me] = ids_send[me]
-
-    bag_i = bag.astype(i32)
-    for d in range(N_DEV):
-        bag_of[d] = jnp.broadcast_to(bag_i[0:MAIN, d : d + 1], (MAIN, 128))
-    bag_t = bag.T.astype(i32)
-    bag_extra[...] = jnp.broadcast_to(bag_t[:, MAIN : MAIN + 1], (128, 128))
-    wait_ids = pltpu.make_async_copy(ids_send.at[pl.ds(0, 127)], ids_recv.at[pl.ds(0, 127)], ids_rsem)
-    wait_ids.wait()
-    ids_recv[...] = jnp.clip(ids_recv[...], 0, ROWS_DEV - 1)
-    smem_copy = pltpu.make_async_copy(ids_recv, ids_smem, smem_sem)
-    smem_copy.start()
-    smem_copy.wait()
+    def send_ids(k, to):
+        pltpu.make_async_remote_copy(
+            ids_send.at[to[0] * N_MEMBER + to[1]], ids_recv.at[k], ids_ssem, ids_rsem.at[k // SERVE],
+            device_id=to, device_id_type=MESH,
+        ).start()
+
+    each_peer(send_ids)
+    ids_recv[0] = ids_send[me]
+
+    def take_ids(c, count):
+        pltpu.make_async_copy(
+            ids_send.at[pl.ds(0, count)], ids_recv.at[pl.ds(0, count)], ids_rsem.at[c]
+        ).wait()
+        at = pl.ds(c * SERVE, SERVE)
+        ids_recv[at] = jnp.clip(ids_recv[at], 0, ROWS_DEV - 1)
+        smem_copy(c).start()
+
+    def smem_copy(c):
+        at = pl.ds(c * SERVE, SERVE)
+        return pltpu.make_async_copy(ids_recv.at[at], ids_smem.at[at], smem_sem.at[c])
+
+    take_ids(0, SERVE - 1)
     table_copy.wait()
 
-    def gather(d, slot):
+    def gather(slot):
         for i in range(MAIN):
-            stage[i : i + 1, :] = table_v[pl.ds(ids_smem[d, 0, i] & (ROWS_DEV - 1), 1), :]
+            stage[i : i + 1, :] = table_v[pl.ds(ids_smem[slot, 0, i] & (ROWS_DEV - 1), 1), :]
         send_main[slot] = stage[...].astype(bf16)
-        send_extra[slot] = table_v[pl.ds(ids_smem[d, 0, MAIN] & (ROWS_DEV - 1), 1), :]
+        send_extra[slot] = table_v[pl.ds(ids_smem[slot, 0, MAIN] & (ROWS_DEV - 1), 1), :]
 
     def rows_copies(k):
-        to = peer(k)
+        to = origin(k)
         return (
             pltpu.make_async_remote_copy(
                 send_main.at[k], recv_main.at[k], row_ssem, rowm_rsem.at[k // GROUP],
@@ -196,16 +204,29 @@
         )
 
     def serve(k, c):
-        to_g, to_m = peer(k)
-        gather(to_g * N_MEMBER + to_m, k)
+        gather(k)
         for copy in rows_copies(k):
             copy.start()
         return c
 
-    lax.fori_loop(1, N_DEV, serve, 0)
-    gather(me, 0)
+    def serve_chunk(c, carry):
+        take_ids(c + 1, SERVE)
+        smem_copy(c).wait()
+        lax.fori_loop(jnp.maximum(c * SERVE, 1), c * SERVE + SERVE, serve, 0)
+        return carry
+
+    lax.fori_loop(0, N_DEV // SERVE - 1, serve_chunk, 0)
+    smem_copy(N_DEV // SERVE - 1).wait()
+    lax.fori_loop(N_DEV - SERVE, N_DEV, serve, 0)
+    gather(0)
     recv_main[0] = send_main[0]
     recv_extra[0] = send_extra[0]
+
+    bag_i = bag.astype(i32)
+    for d in range(N_DEV):
+        bag_of[d] = jnp.broadcast_to(bag_i[0:MAIN, d : d + 1], (MAIN, 128))
+    bag_t = bag.T.astype(i32)
+    bag_extra[...] = jnp.broadcast_to(bag_t[:, MAIN : MAIN + 1], (128, 128))
 
     top_in[...] = jnp.zeros_like(top_in)
     top_in[0:DENSE, :] = x_ref[...]
@@ -242,7 +263,7 @@
 
     def pool_main(q):
         for i in range(GROUP):
-            from_g, from_m = origin(q * GROUP + i)
+            from_g, from_m = peer(q * GROUP + i)
             st[pl.ds(i * MAIN, MAIN), :] = one_hot(bag_of[from_g * N_MEMBER + from_m])
         rows = recv_main[pl.ds(q * GROUP, GROUP)].reshape(GROUP * MAIN, E)
         pooled[...] += dot(rows, st[...], TN)
@@ -266,7 +287,7 @@
         send_extra.at[pl.ds(0, 127)], recv_extra.at[pl.ds(0, 127)], rowe_rsem
     ).wait()
     for k in range(N_DEV):
-        from_g, from_m = origin(k)
+        from_g, from_m = peer(k)
         hid[pl.ds(from_g * N_MEMBER + from_m, 1), :] = recv_extra[k]
     pooled[...] += dot(hid[0:128, :].astype(bf16), one_hot(bag_extra[...]), TN)
 
@@ -307,11 +328,11 @@
         to_g, to_m = peer(k)
         return (
             pltpu.make_async_remote_copy(
-                send_main.at[k], gmain_out.at[me], g_ssem, gm_rsem,
+                send_main.at[k], gmain_out.at[k], g_ssem, gm_rsem,
                 device_id=(to_g, to_m), device_id_type=MESH,
             ),
             pltpu.make_async_remote_copy(
-                send_extra.at[to_g * N_MEMBER + to_m], gextra_out.at[me], g_esem, ge_rsem,
+                send_extra.at[to_g * N_MEMBER + to_m], gextra_out.at[k], g_esem, ge_rsem,
                 device_id=(to_g, to_m), device_id_type=MESH,
             ),
         )
@@ -337,80 +358,107 @@
         return c
 
     lax.fori_loop(1, N_DEV // GROUP, expand_step, 0)
-    gmain_out[me] = send_main[0]
-    gextra_out[me] = send_extra[me]
+    own_copy = pltpu.make_async_copy(send_main.at[0], gmain_out.at[0], own_sem)
+    own_copy.start()
+    gextra_out[0] = send_extra[me]
     ids_out[...] = ids_recv[...]
 
-    flat_out[...] = jnp.zeros_like(flat_out)
-    g_t0 = dot3(top_h, dup_h, NT_).astype(bf16)
+    flat[...] = jnp.zeros_like(flat)
+    g_t0 = dot3(top_h, dup_h, NT_)
     for c in range(8):
-        flat_out[OFF_TOP0 + c * TOP0_ROWS : OFF_TOP0 + (c + 1) * TOP0_ROWS, :] = g_t0[
+        flat[OFF_TOP0 + c * TOP0_ROWS : OFF_TOP0 + (c + 1) * TOP0_ROWS, :] = g_t0[
             0:TOP0_ROWS, 128 * c : 128 * (c + 1)
         ]
     lg_h = halves(jnp.broadcast_to(lg, (8, 128)))
     g_t1 = dot3(lg_h, halves(hid[...]), NT_)[0:1]
     g_t1 = jnp.concatenate([g_t1[:, 128 * c : 128 * (c + 1)] for c in range(8)], axis=0)
-    flat_out[OFF_TOP1 : OFF_TOP1 + 16, :] = jnp.concatenate([g_t1, g_t1], axis=0).astype(bf16)
+    flat[OFF_TOP1 : OFF_TOP1 + 16, :] = jnp.concatenate([g_t1, g_t1], axis=0)
     d_bp = halves((d_top[0:128] + d_z[0]) * d3)
-    flat_out[OFF_BOT2 : OFF_BOT2 + BOT2, :] = dot3(h2_h, d_bp, NT_).astype(bf16)
+    flat[OFF_BOT2 : OFF_BOT2 + BOT2, :] = dot3(h2_h, d_bp, NT_)
     d_h2p = halves(dot3(w2_h, d_bp, NN) * d2)
-    g_b1 = dot3(h1_h, d_h2p, NT_).astype(bf16)
+    g_b1 = dot3(h1_h, d_h2p, NT_)
     for c in range(2):
-        flat_out[OFF_BOT1 + c * BOT1 : OFF_BOT1 + (c + 1) * BOT1, :] = g_b1[:, 128 * c : 128 * (c + 1)]
+        flat[OFF_BOT1 + c * BOT1 : OFF_BOT1 + (c + 1) * BOT1, :] = g_b1[:, 128 * c : 128 * (c + 1)]
     d_h1p = halves(dot3(w1_h, d_h2p, NN) * d1)
-    g_b0 = dot3(x_h, d_h1p, NT_)[0:16].astype(bf16)
+    g_b0 = dot3(x_h, d_h1p, NT_)[0:16]
     for c in range(4):
-        flat_out[OFF_BOT0 + c * 16 : OFF_BOT0 + (c + 1) * 16, :] = g_b0[:, 128 * c : 128 * (c + 1)]
-
+        flat[OFF_BOT0 + c * 16 : OFF_BOT0 + (c + 1) * 16, :] = g_b0[:, 128 * c : 128 * (c + 1)]
+
+    core = g % 2
+    half_copy = pltpu.make_async_remote_copy(
+        flat.at[pl.ds(pl.multiple_of((1 - core) * HALF, HALF), HALF)], flat_half, half_ssem, half_rsem,
+        device_id=(g + 1 - 2 * core, m), device_id_type=MESH,
+    )
+    half_copy.start()
+    half_copy.wait()
+    own_half = flat[pl.ds(pl.multiple_of(core * HALF, HALF), HALF), :]
+    flat_out[...] = (own_half + flat_half[...]).astype(bf16)
+
+    own_copy.wait()
     pltpu.make_async_copy(ids_send.at[pl.ds(0, 127)], ids_recv.at[pl.ds(0, 127)], ids_ssem).wait()
     pltpu.make_async_copy(send_main.at[pl.ds(0, 127)], recv_main.at[pl.ds(0, 127)], g_ssem).wait()
     pltpu.make_async_copy(send_extra.at[pl.ds(0, 127)], recv_extra.at[pl.ds(0, 127)], g_esem).wait()
-    pltpu.make_async_copy(send_main.at[pl.ds(0, 127)], gmain_out.at[pl.ds(0, 127)], gm_rsem).wait()
+    pltpu.make_async_copy(send_main.at[pl.ds(1, 127)], gmain_out.at[pl.ds(1, 127)], gm_rsem).wait()
     pltpu.make_async_copy(send_extra.at[pl.ds(0, 127)], gextra_out.at[pl.ds(0, 127)], ge_rsem).wait()
 
 
-WAYS = 4
-
-
-def scatter_kernel(ids_ref, gmain_ref, gextra_ref, table_ref, new_ref, change_ref, sums, stage):
+WAYS = 8
+CHUNK = 512
+
+
+def scatter_kernel(ids_ref, gmain_hbm, gextra_ref, table_hbm, new_hbm, change_hbm,
+                   sums, stage, gmain, table, change, gmain_sem, table_sem, new_sem, change_sem):
+    gmain_copy = pltpu.make_async_copy(gmain_hbm, gmain, gmain_sem)
+    gmain_copy.start()
+    table_copy = pltpu.make_async_copy(table_hbm, table, table_sem)
+    table_copy.start()
     sums[...] = jnp.zeros_like(sums)
+    stage[...] = jnp.zeros_like(stage)
+    gmain_copy.wait()
 
     def source(s, c):
-        stage[0:MAIN, :] = gmain_ref[s].astype(f32)
+        stage[0:MAIN, :] = gmain[s].astype(f32)
         stage[MAIN : MAIN + 1, :] = gextra_ref[s]
         count = ids_ref[s, 0, 127]
 
-        def batch(b, c):
-            first = b * 8
-            for half in range(0, 8, WAYS):
-                rows, total = [], []
-                for i in range(WAYS):
-                    r = ids_ref[s, 0, first + half + i]
-                    rows.append(r)
-                    total.append(
-                        sums[i, pl.ds(r, 1), :] + stage[pl.ds(first + half + i, 1), :]
-                    )
-                for i in range(WAYS):
-                    sums[i, pl.ds(rows[i], 1), :] = total[i]
-            return c
-
-        lax.fori_loop(0, (count + 7) // 8, batch, 0)
+        def fetch(first):
+            return (
+                [ids_ref[s, 0, first + i] for i in range(WAYS)],
+                [stage[pl.ds(first + i, 1), :] for i in range(WAYS)],
+            )
+
+        def batch(b, carry):
+            rows, terms = carry
+            total = [sums[i, pl.ds(rows[i], 1), :] + terms[i] for i in range(WAYS)]
+            ahead = fetch((b + 1) * WAYS)
+            for i in range(WAYS):
+                sums[i, pl.ds(rows[i], 1), :] = total[i]
+            return ahead
+
+        lax.fori_loop(0, (count + WAYS - 1) // WAYS, batch, fetch(0))
         return c
 
-    stage[...] = jnp.zeros_like(stage)
     lax.fori_loop(0, N_DEV, source, 0)
+    table_copy.wait()
 
     def finish(b, c):
-        at = pl.ds(pl.multiple_of(b * 256, 256), 256)
-        total = sums[0, at, :]
-        for i in range(1, WAYS):
-            total = total + sums[i, at, :]
-        total = -embed_rate * total
-        new_ref[at, :] = table_ref[at, :] + total
-        change_ref[at, :] = total.astype(bf16)
+        start = pl.multiple_of(b * CHUNK, CHUNK)
+        for r in range(0, CHUNK, 64):
+            at = pl.ds(pl.multiple_of(start + r, 64), 64)
+            total = sums[0, at, :]
+            for i in range(1, WAYS):
+                total = total + sums[i, at, :]
+            total = -embed_rate * total
+            table[at, :] = table[at, :] + total
+            change[at, :] = total.astype(bf16)
+        at = pl.ds(start, CHUNK)
+        pltpu.make_async_copy(table.at[at], new_hbm.at[at], new_sem).start()
+        pltpu.make_async_copy(change.at[at], change_hbm.at[at], change_sem).start()
         return c
 
-    lax.fori_loop(0, ROWS_DEV // 256, finish, 0)
+    lax.fori_loop(0, ROWS_DEV // CHUNK, finish, 0)
+    pltpu.make_async_copy(table, new_hbm, new_sem).wait()
+    pltpu.make_async_copy(change, change_hbm, change_sem).wait()
 
 
 def member_peer(k, sign):
@@ -422,10 +470,13 @@
     return ((x + kx) % 4) * 4 + (y + ky) % 4
 
 
+CUT = (5, 9, 13)
+
+
 def parity_kernel(
     change_ref, parity_ref, flat_ref,
-    new_ref, g0_ref, g1_ref, g2_ref, gt0_ref, gt1_ref,
-    pieces, part_z, sum_z, part_xy, sum_xy, all_xy, all_z_send, all_z,
+    new_ref, all_z,
+    pieces, part_z, sum_z, part_xy, sum_xy, all_xy, all_z_send,
     ch_ssem, ch_rsem, rz_ssem, rz_rsem, rx_ssem, rx_rsem, ax_ssem, ax_rsem, az_ssem, az_rsem,
 ):
     g, m = lax.axis_index("group"), lax.axis_index("member")
@@ -448,11 +499,13 @@
             (g, to),
         )
 
+    z, core = g // 2, g % 2
+
     def rz_copy(j):
-        to = (g + j) % N_GROUP
+        to = (z + j) % 4
         return remote(
             flat_ref.at[pl.ds(pl.multiple_of(to * PIECE, PIECE), PIECE)], part_z.at[j], rz_ssem.at[j], rz_rsem.at[j],
-            (to, m),
+            (to * 2 + core, m),
         )
 
     def rx_copy(k):
@@ -465,21 +518,23 @@
     def ax_copy(k):
         return remote(sum_xy, all_xy.at[m], ax_ssem.at[k], ax_rsem.at[k], (g, member_peer(k, 1)))
 
+    place = core * 4 + z
+
     def az_copy(j):
-        return remote(all_z_send, all_z.at[g], az_ssem.at[j], az_rsem.at[j], ((g + j) % N_GROUP, m))
-
-    for j in range(1, N_GROUP):
+        return remote(all_z_send, all_z.at[place], az_ssem.at[j], az_rsem.at[j], ((g + j) % N_GROUP, m))
+
+    for j in range(1, 4):
         rz_copy(j).start()
-    for k in range(1, 6):
+    for k in range(1, CUT[0]):
         change_copy(k).start()
-    total = flat_ref[pl.ds(pl.multiple_of(g * PIECE, PIECE), PIECE), :].astype(f32)
-    for j in range(1, N_GROUP):
+    total = flat_ref[pl.ds(pl.multiple_of(z * PIECE, PIECE), PIECE), :].astype(f32)
+    for j in range(1, 4):
         rz_copy(j).wait()
         total = total + part_z[j].astype(f32)
     sum_z[...] = total
     for k in range(1, N_MEMBER):
         rx_copy(k).start()
-    for k in range(6, 11):
+    for k in range(CUT[0], CUT[1]):
         change_copy(k).start()
     total = sum_z[pl.ds(pl.multiple_of(m * SMALL, SMALL), SMALL), :]
     for k in range(1, N_MEMBER):
@@ -488,7 +543,7 @@
     sum_xy[...] = total
     for k in range(1, N_MEMBER):
         ax_copy(k).start()
-    for k in range(11, N_MEMBER):
+    for k in range(CUT[1], CUT[2]):
         change_copy(k).start()
     all_xy[m] = total
     for k in range(1, N_MEMBER):
@@ -496,6 +551,8 @@
     all_z_send[...] = all_xy[...].reshape(PIECE, E).astype(bf16)
     for j in range(1, N_GROUP):
         az_copy(j).start()
+    for k in range(CUT[2], N_MEMBER):
+        change_copy(k).start()
 
     def weights(k):
         source = member_peer(k, -1).astype(f32) / N_MEMBER
@@ -521,9 +578,13 @@
 
     lax.fori_loop(0, rows // 32, combine, 0)
 
-    all_z[g] = all_z_send[...]
+    all_z[place] = all_z_send[...]
     for j in range(1, N_GROUP):
         az_copy(j).wait()
+
+
+def unpack_kernel(parity_ref, all_z, new_ref, g0_ref, g1_ref, g2_ref, gt0_ref, gt1_ref):
+    new_ref[...] = parity_ref[...]
     for c in range(8):
         gt0_ref[:, 128 * c : 128 * (c + 1)] = piece_rows(all_z, OFF_TOP0 + c * TOP0_ROWS, TOP0_ROWS)[0:TOPIN]
     for c in range(2):
@@ -563,10 +624,10 @@
             sds((N_DEV, 1, 128), i32),
             sds((N_DEV, MAIN, E), bf16),
             sds((N_DEV, 1, E), f32),
-            sds((FLAT, E), bf16),
+            sds((HALF, E), bf16),
         ),
         in_specs=[vmem] * 5 + [anyw] + [vmem] * 5,
-        out_specs=(vmem,) * 4,
+        out_specs=(vmem, anyw, vmem, vmem),
         scratch_shapes=[
             VM((ROWS_DEV, E), f32),
             VM((N_DEV, 1, 128), i32),
@@ -577,6 +638,8 @@
             VM((N_DEV, 1, E), f32),
             VM((N_DEV, MAIN, E), bf16),
             VM((N_DEV, 1, E), f32),
+            VM((32, 128, 256), bf16),
+            VM((32, 512, 256), bf16),
             VM((N_DEV, MAIN, 128), i32),
             VM((128, 128), i32),
             VM((GROUP * MAIN, BAGS), bf16),
@@ -586,7 +649,11 @@
             VM((256, 128), f32),
             VM((TOPH, 128), f32),
             VM((TOPH, 128), f32),
-            dma, dma, dma, dma, dma, dma, dma((N_DEV // GROUP,)), dma, dma, dma, dma, dma,
+            dma, dma((N_DEV // SERVE,)), dma, dma((N_DEV // SERVE,)), dma, dma, dma((N_DEV // GROUP,)), dma,
+            dma, dma, dma, dma,
+            VM((FLAT, E), f32),
+            VM((HALF, E), f32),
+            dma, dma, dma,
         ],
         compiler_params=pltpu.CompilerParams(
             collective_id=0, has_side_effects=True, vmem_limit_bytes=56 << 20
@@ -598,13 +665,41 @@
     new_table, change = pl.pallas_call(
         scatter_kernel,
         out_shape=(sds((ROWS_DEV, E), f32), sds((ROWS_DEV, E), bf16)),
-        in_specs=[smem, vmem, vmem, vmem],
-        out_specs=(vmem, vmem),
-        scratch_shapes=[VM((WAYS, ROWS_DEV, E), f32), VM((MAIN + 8, E), f32)],
+        in_specs=[smem, anyw, vmem, anyw],
+        out_specs=(anyw, anyw),
+        scratch_shapes=[
+            VM((WAYS, ROWS_DEV, E), f32),
+            VM((MAIN + 16, E), f32),
+            VM((N_DEV, MAIN, E), bf16),
+            VM((ROWS_DEV, E), f32),
+            VM((ROWS_DEV, E), bf16),
+            dma, dma, dma, dma,
+        ],
         compiler_params=pltpu.CompilerParams(vmem_limit_bytes=56 << 20),
     )(ids, gmain, gextra, table)
+    parity_sum, all_z = pl.pallas_call(
+        parity_kernel,
+        out_shape=(sds(parity.shape, f32), sds((N_GROUP, PIECE, E), bf16)),
+        in_specs=[vmem] * 3,
+        out_specs=(vmem, vmem),
+        scratch_shapes=[
+            VM((N_MEMBER, ROWS_DEV // N_MEMBER, E), bf16),
+            VM((4, PIECE, E), bf16),
+            VM((PIECE, E), f32),
+            VM((N_MEMBER, SMALL, E), f32),
+            VM((SMALL, E), f32),
+            VM((N_MEMBER, SMALL, E), f32),
+            VM((PIECE, E), bf16),
+            dma((N_MEMBER,)), dma((N_MEMBER,)), dma((4,)), dma((4,)),
+            dma((N_MEMBER,)), dma((N_MEMBER,)), dma((N_MEMBER,)), dma((N_MEMBER,)),
+            dma((N_GROUP,)), dma((N_GROUP,)),
+        ],
+        compiler_params=pltpu.CompilerParams(
+            collective_id=1, has_side_effects=True, vmem_limit_bytes=56 << 20
+        ),
+    )(change, parity, flat)
     new_parity, g0, g1, g2, gt0, gt1 = pl.pallas_call(
-        parity_kernel,
+        unpack_kernel,
         out_shape=(
             sds(parity.shape, f32),
             sds((DENSE, BOT1), f32),
@@ -613,25 +708,10 @@
             sds((TOPIN, TOPH), f32),
             sds((1, TOPH), f32),
         ),
-        in_specs=[vmem] * 3,
+        in_specs=[vmem] * 2,
         out_specs=(vmem,) * 6,
-        scratch_shapes=[
-            VM((N_MEMBER, ROWS_DEV // N_MEMBER, E), bf16),
-            VM((N_GROUP, PIECE, E), bf16),
-            VM((PIECE, E), f32),
-            VM((N_MEMBER, SMALL, E), f32),
-            VM((SMALL, E), f32),
-            VM((N_MEMBER, SMALL, E), f32),
-            VM((PIECE, E), bf16),
-            VM((N_GROUP, PIECE, E), bf16),
-            dma((N_MEMBER,)), dma((N_MEMBER,)), dma((N_GROUP,)), dma((N_GROUP,)),
-            dma((N_MEMBER,)), dma((N_MEMBER,)), dma((N_MEMBER,)), dma((N_MEMBER,)),
-            dma((N_GROUP,)), dma((N_GROUP,)),
-        ],
-        compiler_params=pltpu.CompilerParams(
-            collective_id=1, has_side_effects=True, vmem_limit_bytes=56 << 20
-        ),
-    )(change, parity, flat)
+        compiler_params=pltpu.CompilerParams(vmem_limit_bytes=32 << 20),
+    )(parity_sum, all_z)
     return new_table, new_parity, g0, g1, g2, gt0, gt1.reshape(TOPH)
 
 

time: 210 us -> 180 us (0.86)
  Pallas kernels: 199 us -> 177 us
  local copies, waits for them, and re-layouts: 9.97 us -> 2.17 us
    pallas_call x1, Pallas kernels: 122 us -> 104 us  [body(): pl.pallas_call(exchange_kernel, out_shape=(sds((N_DEV, 1, 128), i32), sds...]
    pallas_call x1 -> x2, Pallas kernels: 51.5 us -> 43 us  [the longest x1 41.7 us: body(): pl.pallas_call(parity_kernel, out_shape=(sds(parity.shape, f32), sds((N_G...]
    unnamed x6 -> x4, local copies, waits for them, and re-layouts: 9.97 us -> 2.17 us
    pallas_call x1, Pallas kernels: 25 us -> 29.9 us  [body(): pl.pallas_call(scatter_kernel, out_shape=(sds((ROWS_DEV, E), f32), sds((R...]
where the time goes in v2:
time: 180 us
  Pallas kernels  177 us (98%)
  local copies, waits for them, and re-layouts  2.17 us (1%)
    pallas_call x1, Pallas kernels, body(): pl.pallas_call(exchange_kernel, out_shape=(sds((N_DEV, 1, 128), i32), sds...  104 us
    pallas_call x1, Pallas kernels, body(): pl.pallas_call(parity_kernel, out_shape=(sds(parity.shape, f32), sds((N_G...  41.7 us
    pallas_call x1, Pallas kernels, body(): pl.pallas_call(scatter_kernel, out_shape=(sds((ROWS_DEV, E), f32), sds((R...  29.9 us

profile of v2, /device:TPU:1, one launch (start us, length us, event | category | flops | bytes accessed | tf_op | source)
XLA Modules:
  0.0 180.0 jit_solution(4644922219063397881)
XLA Ops:
  0.6 104.2 %shard_map.171 = (s32[128,1,128]{2,1,0:T(1,128)}, bf16[128,96,128]{2,1,0:T(8,128)(2,1)}, f32[128,1,128]{2,1,0:T(1,128)}, bf16[1536,128]{1,0:T(8,128)(2,1)}) custom-call(s32[64,128]{1,0:T(8,128)} %bitcast.11, s32[64,128]{1,0:T(8,128)} %bitcast.12, s32[8,128]{1,0:T(8,128)} %bitcast.14, f32[13,128]{1,0:T(8,128)} %bitcast.13, f32[1,128]{1,0:T(1,128)} %bitcast.16, ...), custom_call_target="tpu_custom_call" | custom-call | tf_op jit(solution)/shard_map/pallas_call | solution.py:621
  104.9 29.9 %shard_map.172 = (f32[8192,128]{1,0:T(8,128)}, bf16[8192,128]{1,0:T(8,128)(2,1)}) custom-call(s32[128,1,128]{2,1,0:T(1,128)} %get-tuple-element.21.ids_ref, bf16[128,96,128]{2,1,0:T(8,128)(2,1)} %get-tuple-element.22.gmain_hbm, f32[128,1,128]{2,1,0:T(1,128)} %get-tuple-element.23.gextra_ref, f32[8192,128]{1,0:T(8,128)} %table_hbm.3), custom_call_target="tpu_custom_call" | custom-call | tf_op jit(solution)/shard_map/pallas_call | solution.py:665
  134.8 41.7 %shard_map.173 = (f32[512,256]{1,0:T(8,128)}, bf16[8,384,128]{2,1,0:T(8,128)(2,1)}) custom-call(bf16[8192,128]{1,0:T(8,128)(2,1)} %get-tuple-element.25.change_ref, f32[512,256]{1,0:T(8,128)} %parity_ref.1, bf16[1536,128]{1,0:T(8,128)(2,1)} %get-tuple-element.26.flat_ref), custom_call_target="tpu_custom_call" | custom-call | tf_op jit(solution)/shard_map/pallas_call | solution.py:680
  176.5 0.0 copy-start
  176.5 1.1 copy-done
  177.7 0.0 copy-start.1
  177.7 1.0 copy-done.1
  178.7 1.3 shard_map.174
Async XLA Ops:
  176.5 1.1 copy-start
  177.7 1.0 copy-start.1

commit v3 on v2

--- a/solution.py
+++ b/solution.py
@@ -108,12 +108,13 @@
 
 
 def exchange_kernel(
-    own_ref, row_ref, len_ref, x_ref, lg_ref, table_hbm, w0_ref, w1_ref, w2_ref, wt0_ref, wt1_ref,
+    own_ref, row_ref, len_ref, x_ref, lg_ref, table_hbm, w0_hbm, w1_hbm, w2_hbm, wt0_hbm, wt1_ref,
     ids_out, gmain_out, gextra_out, flat_out,
     table_v, ids_send, ids_recv, ids_smem, stage, send_main, send_extra, recv_main, recv_extra,
-    hits, vals, bag_of, bag_extra, st, pooled, pg, wt0_p, top_in, hid, dup,
+    hits, vals, bag_of, bag_extra, st, st_extra, pooled, pg, wt0_p, top_in, hid, dup,
     table_sem, smem_sem, ids_ssem, ids_rsem, row_ssem, row_esem, rowm_rsem, rowe_rsem,
     g_ssem, g_esem, gm_rsem, ge_rsem, flat, flat_half, own_sem, half_ssem, half_rsem,
+    w0_ref, w1_ref, w2_ref, wt0_ref, w_sem,
 ):
     g, m = lax.axis_index("group"), lax.axis_index("member")
     me = g * N_MEMBER + m
@@ -121,6 +122,12 @@
     table_copy = pltpu.make_async_copy(table_hbm, table_v, table_sem)
     table_copy.start()
     barrier = pltpu.get_barrier_semaphore()
+    weight_copies = [
+        pltpu.make_async_copy(src, dst, w_sem.at[i])
+        for i, (src, dst) in enumerate([(w0_hbm, w0_ref), (w1_hbm, w1_ref), (w2_hbm, w2_ref), (wt0_hbm, wt0_ref)])
+    ]
+    for copy in weight_copies:
+        copy.start()
 
     each_peer(lambda k, to: pl.semaphore_signal(barrier, 1, device_id=to, device_id_type=MESH))
 
@@ -198,7 +205,7 @@
                 device_id=to, device_id_type=MESH,
             ),
             pltpu.make_async_remote_copy(
-                send_extra.at[k], recv_extra.at[k], row_esem, rowe_rsem,
+                send_extra.at[k], recv_extra.at[k], row_esem, rowe_rsem.at[k // GROUP],
                 device_id=to, device_id_type=MESH,
             ),
         )
@@ -227,6 +234,9 @@
         bag_of[d] = jnp.broadcast_to(bag_i[0:MAIN, d : d + 1], (MAIN, 128))
     bag_t = bag.T.astype(i32)
     bag_extra[...] = jnp.broadcast_to(bag_t[:, MAIN : MAIN + 1], (128, 128))
+
+    for copy in weight_copies:
+        copy.wait()
 
     top_in[...] = jnp.zeros_like(top_in)
     top_in[0:DENSE, :] = x_ref[...]
@@ -265,6 +275,7 @@
         for i in range(GROUP):
             from_g, from_m = peer(q * GROUP + i)
             st[pl.ds(i * MAIN, MAIN), :] = one_hot(bag_of[from_g * N_MEMBER + from_m])
+            hid[pl.ds(from_g * N_MEMBER + from_m, 1), :] = recv_extra[q * GROUP + i]
         rows = recv_main[pl.ds(q * GROUP, GROUP)].reshape(GROUP * MAIN, E)
         pooled[...] += dot(rows, st[...], TN)
 
@@ -272,7 +283,11 @@
         pltpu.make_async_copy(
             send_main.at[pl.ds(0, count)], recv_main.at[pl.ds(0, count)], rowm_rsem.at[q]
         ).wait()
-
+        pltpu.make_async_copy(
+            send_extra.at[pl.ds(0, count)], recv_extra.at[pl.ds(0, count)], rowe_rsem.at[q]
+        ).wait()
+
+    st_extra[...] = one_hot(bag_extra[...])
     pooled[...] = jnp.zeros_like(pooled)
     wait_rows(0, GROUP - 1)
     pool_main(0)
@@ -283,13 +298,7 @@
         return c
 
     lax.fori_loop(1, N_DEV // GROUP, pool_step, 0)
-    pltpu.make_async_copy(
-        send_extra.at[pl.ds(0, 127)], recv_extra.at[pl.ds(0, 127)], rowe_rsem
-    ).wait()
-    for k in range(N_DEV):
-        from_g, from_m = peer(k)
-        hid[pl.ds(from_g * N_MEMBER + from_m, 1), :] = recv_extra[k]
-    pooled[...] += dot(hid[0:128, :].astype(bf16), one_hot(bag_extra[...]), TN)
+    pooled[...] += dot(hid[0:128, :].astype(bf16), st_extra[...], TN)
 
     z = [bottom] + [pooled[:, 128 * t : 128 * (t + 1)] for t in range(NT)]
     for n, (i, j) in enumerate(PAIRS):
@@ -320,22 +329,16 @@
     pltpu.make_async_copy(send_main.at[pl.ds(0, 127)], recv_main.at[pl.ds(0, 127)], row_ssem).wait()
     pltpu.make_async_copy(send_extra.at[pl.ds(0, 127)], recv_extra.at[pl.ds(0, 127)], row_esem).wait()
 
-    extra = dot(one_hot(bag_extra[...]), pg[...], NN)
-    for d in range(N_DEV):
-        send_extra[d] = extra[d : d + 1, :]
-
-    def grad_copies(k):
-        to_g, to_m = peer(k)
-        return (
-            pltpu.make_async_remote_copy(
-                send_main.at[k], gmain_out.at[k], g_ssem, gm_rsem,
-                device_id=(to_g, to_m), device_id_type=MESH,
-            ),
-            pltpu.make_async_remote_copy(
-                send_extra.at[to_g * N_MEMBER + to_m], gextra_out.at[k], g_esem, ge_rsem,
-                device_id=(to_g, to_m), device_id_type=MESH,
-            ),
+    def main_copy(k):
+        return pltpu.make_async_remote_copy(
+            send_main.at[k], gmain_out.at[k], g_ssem, gm_rsem, device_id=peer(k), device_id_type=MESH
         )
+
+    def send_grad_extra(k, to):
+        pltpu.make_async_remote_copy(
+            send_extra.at[to[0] * N_MEMBER + to[1]], gextra_out.at[k], g_esem, ge_rsem,
+            device_id=to, device_id_type=MESH,
+        ).start()
 
     def expand(q):
         for i in range(GROUP):
@@ -345,8 +348,7 @@
         send_main[pl.ds(q * GROUP, GROUP)] = grads.reshape(GROUP, MAIN, E)
 
     def start_grads(k, c):
-        for copy in grad_copies(k):
-            copy.start()
+        main_copy(k).start()
         return c
 
     expand(0)
@@ -357,7 +359,12 @@
         lax.fori_loop(q * GROUP, q * GROUP + GROUP, start_grads, 0)
         return c
 
-    lax.fori_loop(1, N_DEV // GROUP, expand_step, 0)
+    lax.fori_loop(1, N_DEV // GROUP // 2, expand_step, 0)
+    extra = dot(st_extra[...], pg[...], NN)
+    for d in range(N_DEV):
+        send_extra[d] = extra[d : d + 1, :]
+    each_peer(send_grad_extra)
+    lax.fori_loop(N_DEV // GROUP // 2, N_DEV // GROUP, expand_step, 0)
     own_copy = pltpu.make_async_copy(send_main.at[0], gmain_out.at[0], own_sem)
     own_copy.start()
     gextra_out[0] = send_extra[me]
@@ -402,43 +409,53 @@
     pltpu.make_async_copy(send_extra.at[pl.ds(0, 127)], gextra_out.at[pl.ds(0, 127)], ge_rsem).wait()
 
 
-WAYS = 8
+WAYS = 4
+BATCH = 32
 CHUNK = 512
 
 
 def scatter_kernel(ids_ref, gmain_hbm, gextra_ref, table_hbm, new_hbm, change_hbm,
                    sums, stage, gmain, table, change, gmain_sem, table_sem, new_sem, change_sem):
-    gmain_copy = pltpu.make_async_copy(gmain_hbm, gmain, gmain_sem)
-    gmain_copy.start()
+    def gmain_copy(q):
+        at = pl.ds(q * SERVE, SERVE)
+        return pltpu.make_async_copy(gmain_hbm.at[at], gmain.at[at], gmain_sem.at[q])
+
+    for q in range(N_DEV // SERVE):
+        gmain_copy(q).start()
     table_copy = pltpu.make_async_copy(table_hbm, table, table_sem)
     table_copy.start()
     sums[...] = jnp.zeros_like(sums)
-    stage[...] = jnp.zeros_like(stage)
-    gmain_copy.wait()
+
+    def convert(s, c):
+        stage[s, 0:MAIN, :] = gmain[s].astype(f32)
+        stage[s, MAIN : MAIN + 8, :] = jnp.where(iota((8, 128), 0) == 0, gextra_ref[s], 0.0)
+        stage[s, MAIN + 8 : 128, :] = jnp.zeros((24, 128), f32)
+        return c
 
     def source(s, c):
-        stage[0:MAIN, :] = gmain[s].astype(f32)
-        stage[MAIN : MAIN + 1, :] = gextra_ref[s]
         count = ids_ref[s, 0, 127]
 
-        def fetch(first):
-            return (
-                [ids_ref[s, 0, first + i] for i in range(WAYS)],
-                [stage[pl.ds(first + i, 1), :] for i in range(WAYS)],
-            )
-
-        def batch(b, carry):
-            rows, terms = carry
-            total = [sums[i, pl.ds(rows[i], 1), :] + terms[i] for i in range(WAYS)]
-            ahead = fetch((b + 1) * WAYS)
-            for i in range(WAYS):
-                sums[i, pl.ds(rows[i], 1), :] = total[i]
-            return ahead
-
-        lax.fori_loop(0, (count + WAYS - 1) // WAYS, batch, fetch(0))
+        def batch(b, c):
+            first = pl.multiple_of(b * BATCH, BATCH)
+            for h in range(0, BATCH, WAYS):
+                rows = [ids_ref[s, 0, first + h + i] for i in range(WAYS)]
+                total = [
+                    sums[i, pl.ds(rows[i], 1), :] + stage[s, pl.ds(first + h + i, 1), :] for i in range(WAYS)
+                ]
+                for i in range(WAYS):
+                    sums[i, pl.ds(rows[i], 1), :] = total[i]
+            return c
+
+        lax.fori_loop(0, (count + BATCH - 1) // BATCH, batch, 0)
         return c
 
-    lax.fori_loop(0, N_DEV, source, 0)
+    def chunk(q, c):
+        gmain_copy(q).wait()
+        lax.fori_loop(0, SERVE, lambda i, c: convert(q * SERVE + i, c), 0, unroll=4)
+        lax.fori_loop(q * SERVE, q * SERVE + SERVE, source, 0)
+        return c
+
+    lax.fori_loop(0, N_DEV // SERVE, chunk, 0)
     table_copy.wait()
 
     def finish(b, c):
@@ -476,8 +493,8 @@
 def parity_kernel(
     change_ref, parity_ref, flat_ref,
     new_ref, all_z,
-    pieces, part_z, sum_z, part_xy, sum_xy, all_xy, all_z_send,
-    ch_ssem, ch_rsem, rz_ssem, rz_rsem, rx_ssem, rx_rsem, ax_ssem, ax_rsem, az_ssem, az_rsem,
+    pieces, part_z, sum_z, part_xy, sum_xy, all_xy,
+    ch_ssem, ch_rsem, rz_ssem, rz_rsem, rx_ssem, rx_rsem, ax_ssem, ax_rsem, az_ssem, az_rsem, ac_ssem, ac_rsem,
 ):
     g, m = lax.axis_index("group"), lax.axis_index("member")
     barrier = pltpu.get_barrier_semaphore()
@@ -521,7 +538,15 @@
     place = core * 4 + z
 
     def az_copy(j):
-        return remote(all_z_send, all_z.at[place], az_ssem.at[j], az_rsem.at[j], ((g + j) % N_GROUP, m))
+        return remote(
+            all_z.at[place], all_z.at[place], az_ssem.at[j], az_rsem.at[j], ((z + j) % 4 * 2 + core, m)
+        )
+
+    def across_copy(j):
+        slot = core * 4 + (z + 4 - j) % 4
+        return remote(
+            all_z.at[slot], all_z.at[slot], ac_ssem.at[j], ac_rsem.at[j], (z * 2 + 1 - core, m)
+        )
 
     for j in range(1, 4):
         rz_copy(j).start()
@@ -548,9 +573,10 @@
     all_xy[m] = total
     for k in range(1, N_MEMBER):
         ax_copy(k).wait()
-    all_z_send[...] = all_xy[...].reshape(PIECE, E).astype(bf16)
-    for j in range(1, N_GROUP):
+    all_z[place] = all_xy[...].reshape(PIECE, E).astype(bf16)
+    for j in range(1, 4):
         az_copy(j).start()
+    across_copy(0).start()
     for k in range(CUT[2], N_MEMBER):
         change_copy(k).start()
 
@@ -559,32 +585,41 @@
         one = jnp.ones((1, 128), f32)
         return 1.0 / (one + source), 1.0 / (one * 2.0 + source)
 
+    for j in range(1, 4):
+        az_copy(j).wait_recv()
+        across_copy(j).start()
+
+    def add(k, part_of, base_of):
+        first, second = weights(k)
+
+        def step(b, c):
+            at = pl.ds(pl.multiple_of(b * 64, 64), 64)
+            part = part_of(b).astype(f32)
+            new_ref[at, 0:128] = base_of[at, 0:128] + first * part
+            new_ref[at, 128:256] = base_of[at, 128:256] + second * part
+            return c
+
+        lax.fori_loop(0, rows // 64, step, 0)
+
+    add(0, lambda b: change_ref[pl.ds(pl.multiple_of(m * rows + b * 64, 64), 64), :], parity_ref)
     for k in range(1, N_MEMBER):
         change_copy(k).wait()
-    coef = [weights(k) for k in range(N_MEMBER)]
-    own_at = m * rows
-
-    def combine(b, c):
-        at = pl.ds(pl.multiple_of(b * 32, 32), 32)
-        part = change_ref[pl.ds(pl.multiple_of(own_at + b * 32, 32), 32), :].astype(f32)
-        first, second = coef[0][0] * part, coef[0][1] * part
-        for k in range(1, N_MEMBER):
-            part = pieces[k, at, :].astype(f32)
-            first = first + coef[k][0] * part
-            second = second + coef[k][1] * part
-        new_ref[at, 0:128] = parity_ref[at, 0:128] + first
-        new_ref[at, 128:256] = parity_ref[at, 128:256] + second
-        return c
-
-    lax.fori_loop(0, rows // 32, combine, 0)
-
-    all_z[place] = all_z_send[...]
-    for j in range(1, N_GROUP):
-        az_copy(j).wait()
-
-
-def unpack_kernel(parity_ref, all_z, new_ref, g0_ref, g1_ref, g2_ref, gt0_ref, gt1_ref):
-    new_ref[...] = parity_ref[...]
+        add(k, lambda b: pieces[k, pl.ds(pl.multiple_of(b * 64, 64), 64), :], new_ref)
+
+    for j in range(4):
+        if j > 0:
+            az_copy(j).wait_send()
+        across_copy(j).wait()
+
+
+def unpack_kernel(
+    parity_hbm, all_z_hbm, new_hbm, g0_ref, g1_ref, g2_ref, gt0_ref, gt1_ref, all_z, parity_sem, all_z_sem
+):
+    parity_copy = pltpu.make_async_copy(parity_hbm, new_hbm, parity_sem)
+    parity_copy.start()
+    all_z_copy = pltpu.make_async_copy(all_z_hbm, all_z, all_z_sem)
+    all_z_copy.start()
+    all_z_copy.wait()
     for c in range(8):
         gt0_ref[:, 128 * c : 128 * (c + 1)] = piece_rows(all_z, OFF_TOP0 + c * TOP0_ROWS, TOP0_ROWS)[0:TOPIN]
     for c in range(2):
@@ -595,6 +630,7 @@
     top1 = piece_rows(all_z, OFF_TOP1, 16)
     for c in range(8):
         gt1_ref[:, 128 * c : 128 * (c + 1)] = top1[c : c + 1, :]
+    parity_copy.wait()
 
 
 def piece_rows(ref, start, count):
@@ -626,7 +662,7 @@
             sds((N_DEV, 1, E), f32),
             sds((HALF, E), bf16),
         ),
-        in_specs=[vmem] * 5 + [anyw] + [vmem] * 5,
+        in_specs=[vmem] * 5 + [anyw] * 5 + [vmem],
         out_specs=(vmem, anyw, vmem, vmem),
         scratch_shapes=[
             VM((ROWS_DEV, E), f32),
@@ -643,17 +679,24 @@
             VM((N_DEV, MAIN, 128), i32),
             VM((128, 128), i32),
             VM((GROUP * MAIN, BAGS), bf16),
+            VM((N_DEV, BAGS), bf16),
             VM((E, BAGS), f32),
             VM((BAGS, E), bf16),
             VM((256, TOPH), f32),
             VM((256, 128), f32),
             VM((TOPH, 128), f32),
             VM((TOPH, 128), f32),
-            dma, dma((N_DEV // SERVE,)), dma, dma((N_DEV // SERVE,)), dma, dma, dma((N_DEV // GROUP,)), dma,
+            dma, dma((N_DEV // SERVE,)), dma, dma((N_DEV // SERVE,)), dma, dma,
+            dma((N_DEV // GROUP,)), dma((N_DEV // GROUP,)),
             dma, dma, dma, dma,
             VM((FLAT, E), f32),
             VM((HALF, E), f32),
             dma, dma, dma,
+            VM((DENSE, BOT1), f32),
+            VM((BOT1, BOT2), f32),
+            VM((BOT2, E), f32),
+            VM((TOPIN, TOPH), f32),
+            dma((4,)),
         ],
         compiler_params=pltpu.CompilerParams(
             collective_id=0, has_side_effects=True, vmem_limit_bytes=56 << 20
@@ -669,11 +712,11 @@
         out_specs=(anyw, anyw),
         scratch_shapes=[
             VM((WAYS, ROWS_DEV, E), f32),
-            VM((MAIN + 16, E), f32),
+            VM((N_DEV, 128, E), f32),
             VM((N_DEV, MAIN, E), bf16),
             VM((ROWS_DEV, E), f32),
             VM((ROWS_DEV, E), bf16),
-            dma, dma, dma, dma,
+            dma((N_DEV // SERVE,)), dma, dma, dma,
         ],
         compiler_params=pltpu.CompilerParams(vmem_limit_bytes=56 << 20),
     )(ids, gmain, gextra, table)
@@ -689,10 +732,9 @@
             VM((N_MEMBER, SMALL, E), f32),
             VM((SMALL, E), f32),
             VM((N_MEMBER, SMALL, E), f32),
-            VM((PIECE, E), bf16),
             dma((N_MEMBER,)), dma((N_MEMBER,)), dma((4,)), dma((4,)),
             dma((N_MEMBER,)), dma((N_MEMBER,)), dma((N_MEMBER,)), dma((N_MEMBER,)),
-            dma((N_GROUP,)), dma((N_GROUP,)),
+            dma((4,)), dma((4,)), dma((4,)), dma((4,)),
         ],
         compiler_params=pltpu.CompilerParams(
             collective_id=1, has_side_effects=True, vmem_limit_bytes=56 << 20
@@ -708,9 +750,10 @@
             sds((TOPIN, TOPH), f32),
             sds((1, TOPH), f32),
         ),
-        in_specs=[vmem] * 2,
-        out_specs=(vmem,) * 6,
-        compiler_params=pltpu.CompilerParams(vmem_limit_bytes=32 << 20),
+        in_specs=[anyw] * 2,
+        out_specs=(anyw,) + (vmem,) * 5,
+        scratch_shapes=[VM((N_GROUP, PIECE, E), bf16), dma, dma],
+        compiler_params=pltpu.CompilerParams(vmem_limit_bytes=60 << 20),
     )(parity_sum, all_z)
     return new_table, new_parity, g0, g1, g2, gt0, gt1.reshape(TOPH)
 

time: 180 us -> 194 us (1.078)
  Pallas kernels: 177 us -> 193 us
  local copies, waits for them, and re-layouts: 2.17 us -> 0 us
    pallas_call x1, Pallas kernels: 1.3 us -> 18.1 us  [body(): pl.pallas_call(unpack_kernel, out_shape=(sds(parity.shape, f32), sds((DEN...]
    pallas_call x1, Pallas kernels: 29.9 us -> 24.4 us  [body(): pl.pallas_call(scatter_kernel, out_shape=(sds((ROWS_DEV, E), f32), sds((R...]
    pallas_call x1, Pallas kernels: 41.7 us -> 46.5 us  [body(): pl.pallas_call(parity_kernel, out_shape=(sds(parity.shape, f32), sds((N_G...]
    unnamed x4 -> x0, local copies, waits for them, and re-layouts: 2.17 us -> none
where the time goes in v3:
time: 194 us; the launch traced here: 193 us
  Pallas kernels  193 us (99%)
    pallas_call x1, Pallas kernels, body(): pl.pallas_call(exchange_kernel, out_shape=(sds((N_DEV, 1, 128), i32), sds...  104 us
    pallas_call x1, Pallas kernels, body(): pl.pallas_call(parity_kernel, out_shape=(sds(parity.shape, f32), sds((N_G...  46.5 us
    pallas_call x1, Pallas kernels, body(): pl.pallas_call(scatter_kernel, out_shape=(sds((ROWS_DEV, E), f32), sds((R...  24.4 us
    pallas_call x1, Pallas kernels, body(): pl.pallas_call(unpack_kernel, out_shape=(sds(parity.shape, f32), sds((DEN...  18.1 us

profile of v3, /device:TPU:1, one launch (start us, length us, event | category | flops | bytes accessed | tf_op | source)
XLA Modules:
  0.0 193.5 jit_solution(1082617780523070700)
XLA Ops:
  0.6 103.7 %shard_map.171 = (s32[128,1,128]{2,1,0:T(1,128)}, bf16[128,96,128]{2,1,0:T(8,128)(2,1)}, f32[128,1,128]{2,1,0:T(1,128)}, bf16[1536,128]{1,0:T(8,128)(2,1)}) custom-call(s32[64,128]{1,0:T(8,128)} %bitcast.11, s32[64,128]{1,0:T(8,128)} %bitcast.12, s32[8,128]{1,0:T(8,128)} %bitcast.14, f32[13,128]{1,0:T(8,128)} %bitcast.13, f32[1,128]{1,0:T(1,128)} %bitcast.16, ...), custom_call_target="tpu_custom_call" | custom-call | tf_op jit(solution)/shard_map/pallas_call | solution.py:657
  104.3 24.4 %shard_map.172 = (f32[8192,128]{1,0:T(8,128)}, bf16[8192,128]{1,0:T(8,128)(2,1)}) custom-call(s32[128,1,128]{2,1,0:T(1,128)} %get-tuple-element.21.ids_ref, bf16[128,96,128]{2,1,0:T(8,128)(2,1)} %get-tuple-element.22.gmain_hbm, f32[128,1,128]{2,1,0:T(1,128)} %get-tuple-element.23.gextra_ref, f32[8192,128]{1,0:T(8,128)} %table_hbm.3), custom_call_target="tpu_custom_call" | custom-call | tf_op jit(solution)/shard_map/pallas_call | solution.py:708
  128.7 46.5 %shard_map.173 = (f32[512,256]{1,0:T(8,128)}, bf16[8,384,128]{2,1,0:T(8,128)(2,1)}) custom-call(bf16[8192,128]{1,0:T(8,128)(2,1)} %get-tuple-element.25.change_ref, f32[512,256]{1,0:T(8,128)} %parity_ref.1, bf16[1536,128]{1,0:T(8,128)(2,1)} %get-tuple-element.26.flat_ref), custom_call_target="tpu_custom_call" | custom-call | tf_op jit(solution)/shard_map/pallas_call | solution.py:723
  175.2 18.1 %shard_map.174 = (f32[512,256]{1,0:T(8,128)}, f32[13,512]{1,0:T(8,128)}, f32[512,256]{1,0:T(8,128)}, f32[256,128]{1,0:T(8,128)}, f32[164,1024]{1,0:T(8,128)}, /*index=5*/f32[1,1024]{1,0:T(1,128)}) custom-call(f32[512,256]{1,0:T(8,128)} %get-tuple-element.27.parity_hbm, bf16[8,384,128]{2,1,0:T(8,128)(2,1)} %get-tuple-element.28.all_z_hbm), custom_call_target="tpu_custom_call" | custom-call | tf_op jit(solution)/shard_map/pallas_call | solution.py:743

commit v4 on v3

--- a/solution.py
+++ b/solution.py
@@ -134,7 +134,7 @@
     upper = (iota((256, 384), 0) < iota((256, 384), 1)).astype(bf16)
     dev_of = iota((128, 256), 0)
     lane = iota((1, 128), 1)
-    bag_lo = jnp.concatenate([lane, lane], axis=1).astype(f32).astype(bf16)
+    bag_lo = (jnp.concatenate([lane, lane], axis=1) + 128).astype(f32).astype(bf16)
 
     def place(j, count):
         t = j // 4
@@ -150,21 +150,22 @@
         pos = jnp.sum(before * hit, axis=0, keepdims=True).astype(i32)
         at = (pos == dev_of).astype(f32).astype(bf16)
         hits[j] = hit_b
-        vals[j, 0:128, :] = at * (row // 128).astype(f32).astype(bf16)
-        vals[j, 128:256, :] = at * (row % 128).astype(f32).astype(bf16)
-        vals[j, 256:384, :] = at * (t + 1).astype(f32).astype(bf16)
-        vals[j, 384:512, :] = at * bag_lo
+        vals[j, 0:128, :] = at * (row // 32).astype(f32).astype(bf16)
+        vals[j, 128:256, :] = at * (row % 32 * 8 + t).astype(f32).astype(bf16)
+        vals[j, 256:384, :] = at * bag_lo
         return count + ranks[:, 256:384]
 
     count = lax.fori_loop(0, 32, place, jnp.zeros((128, 128), f32), unroll=4)
     acc = dot(vals[0], hits[0], NT_)
     for j in range(1, 32):
         acc = acc + dot(vals[j], hits[j], NT_)
-    ids = (acc[0:128] * 128.0 + acc[128:256]).T
+    mixed = acc[128:256].astype(i32)
+    ids = (acc[0:128] * 32.0 + (mixed // 8).astype(f32)).T
     ids = jnp.where(iota((128, 128), 1) == 127, count, ids).astype(i32)
     for d in range(N_DEV):
         ids_send[d] = ids[d : d + 1, :]
-    bag = acc[256:384] * 128.0 + acc[384:512] - 128.0
+    sample = acc[256:384] - 128.0
+    bag = jnp.where(sample >= 0.0, (mixed % 8).astype(f32) * 128.0 + sample, -1.0)
     pl.semaphore_wait(barrier, N_DEV - 1)
 
     def send_ids(k, to):
@@ -613,12 +614,16 @@
 
 
 def unpack_kernel(
-    parity_hbm, all_z_hbm, new_hbm, g0_ref, g1_ref, g2_ref, gt0_ref, gt1_ref, all_z, parity_sem, all_z_sem
+    parity_hbm, all_z_hbm, new_hbm, g0_ref, g1_ref, g2_ref, gt0_ref, gt1_ref,
+    all_z, parity, parity_sem, all_z_sem, new_sem,
 ):
-    parity_copy = pltpu.make_async_copy(parity_hbm, new_hbm, parity_sem)
+    parity_copy = pltpu.make_async_copy(parity_hbm, parity, parity_sem)
     parity_copy.start()
     all_z_copy = pltpu.make_async_copy(all_z_hbm, all_z, all_z_sem)
     all_z_copy.start()
+    parity_copy.wait()
+    new_copy = pltpu.make_async_copy(parity, new_hbm, new_sem)
+    new_copy.start()
     all_z_copy.wait()
     for c in range(8):
         gt0_ref[:, 128 * c : 128 * (c + 1)] = piece_rows(all_z, OFF_TOP0 + c * TOP0_ROWS, TOP0_ROWS)[0:TOPIN]
@@ -630,7 +635,7 @@
     top1 = piece_rows(all_z, OFF_TOP1, 16)
     for c in range(8):
         gt1_ref[:, 128 * c : 128 * (c + 1)] = top1[c : c + 1, :]
-    parity_copy.wait()
+    new_copy.wait()
 
 
 def piece_rows(ref, start, count):
@@ -675,7 +680,7 @@
             VM((N_DEV, MAIN, E), bf16),
             VM((N_DEV, 1, E), f32),
             VM((32, 128, 256), bf16),
-            VM((32, 512, 256), bf16),
+            VM((32, 384, 256), bf16),
             VM((N_DEV, MAIN, 128), i32),
             VM((128, 128), i32),
             VM((GROUP * MAIN, BAGS), bf16),
@@ -752,7 +757,7 @@
         ),
         in_specs=[anyw] * 2,
         out_specs=(anyw,) + (vmem,) * 5,
-        scratch_shapes=[VM((N_GROUP, PIECE, E), bf16), dma, dma],
+        scratch_shapes=[VM((N_GROUP, PIECE, E), bf16), VM(parity.shape, f32), dma, dma, dma],
         compiler_params=pltpu.CompilerParams(vmem_limit_bytes=60 << 20),
     )(parity_sum, all_z)
     return new_table, new_parity, g0, g1, g2, gt0, gt1.reshape(TOPH)

time: 194 us -> 178 us (0.918)
  Pallas kernels: 193 us -> 176 us
    pallas_call x1, Pallas kernels: 18.1 us -> 2.93 us  [body(): pl.pallas_call(unpack_kernel, out_shape=(sds(parity.shape, f32), sds((DEN...]
where the time goes in v4:
time: 178 us; the launch traced here: 177 us
  Pallas kernels  176 us (99%)
    pallas_call x1, Pallas kernels, body(): pl.pallas_call(exchange_kernel, out_shape=(sds((N_DEV, 1, 128), i32), sds...  103 us
    pallas_call x1, Pallas kernels, body(): pl.pallas_call(parity_kernel, out_shape=(sds(parity.shape, f32), sds((N_G...  46.1 us
    pallas_call x1, Pallas kernels, body(): pl.pallas_call(scatter_kernel, out_shape=(sds((ROWS_DEV, E), f32), sds((R...  23.9 us

profile of v4, /device:TPU:1, one launch (start us, length us, event | category | flops | bytes accessed | tf_op | source)
XLA Modules:
  0.0 176.8 jit_solution(2131197366099801555)
XLA Ops:
  0.6 103.0 %shard_map.171 = (s32[128,1,128]{2,1,0:T(1,128)}, bf16[128,96,128]{2,1,0:T(8,128)(2,1)}, f32[128,1,128]{2,1,0:T(1,128)}, bf16[1536,128]{1,0:T(8,128)(2,1)}) custom-call(s32[64,128]{1,0:T(8,128)} %bitcast.11, s32[64,128]{1,0:T(8,128)} %bitcast.12, s32[8,128]{1,0:T(8,128)} %bitcast.14, f32[13,128]{1,0:T(8,128)} %bitcast.13, f32[1,128]{1,0:T(1,128)} %bitcast.16, ...), custom_call_target="tpu_custom_call" | custom-call | tf_op jit(solution)/shard_map/pallas_call | solution.py:662
  103.7 23.9 %shard_map.172 = (f32[8192,128]{1,0:T(8,128)}, bf16[8192,128]{1,0:T(8,128)(2,1)}) custom-call(s32[128,1,128]{2,1,0:T(1,128)} %get-tuple-element.21.ids_ref, bf16[128,96,128]{2,1,0:T(8,128)(2,1)} %get-tuple-element.22.gmain_hbm, f32[128,1,128]{2,1,0:T(1,128)} %get-tuple-element.23.gextra_ref, f32[8192,128]{1,0:T(8,128)} %table_hbm.3), custom_call_target="tpu_custom_call" | custom-call | tf_op jit(solution)/shard_map/pallas_call | solution.py:713
  127.6 46.1 %shard_map.173 = (f32[512,256]{1,0:T(8,128)}, bf16[8,384,128]{2,1,0:T(8,128)(2,1)}) custom-call(bf16[8192,128]{1,0:T(8,128)(2,1)} %get-tuple-element.25.change_ref, f32[512,256]{1,0:T(8,128)} %parity_ref.1, bf16[1536,128]{1,0:T(8,128)(2,1)} %get-tuple-element.26.flat_ref), custom_call_target="tpu_custom_call" | custom-call | tf_op jit(solution)/shard_map/pallas_call | solution.py:728
  173.8 2.9 %shard_map.174 = (f32[512,256]{1,0:T(8,128)}, f32[13,512]{1,0:T(8,128)}, f32[512,256]{1,0:T(8,128)}, f32[256,128]{1,0:T(8,128)}, f32[164,1024]{1,0:T(8,128)}, /*index=5*/f32[1,1024]{1,0:T(1,128)}) custom-call(f32[512,256]{1,0:T(8,128)} %get-tuple-element.27.parity_hbm, bf16[8,384,128]{2,1,0:T(8,128)(2,1)} %get-tuple-element.28.all_z_hbm), custom_call_target="tpu_custom_call" | custom-call | tf_op jit(solution)/shard_map/pallas_call | solution.py:748

commit v5 on v4

--- a/solution.py
+++ b/solution.py
@@ -115,6 +115,7 @@
     table_sem, smem_sem, ids_ssem, ids_rsem, row_ssem, row_esem, rowm_rsem, rowe_rsem,
     g_ssem, g_esem, gm_rsem, ge_rsem, flat, flat_half, own_sem, half_ssem, half_rsem,
     w0_ref, w1_ref, w2_ref, wt0_ref, w_sem,
+    flat_z, part_z, sum_z, part_xy, rz_ssem, rz_rsem, rx_ssem, rx_rsem,
 ):
     g, m = lax.axis_index("group"), lax.axis_index("member")
     me = g * N_MEMBER + m
@@ -365,12 +366,6 @@
     for d in range(N_DEV):
         send_extra[d] = extra[d : d + 1, :]
     each_peer(send_grad_extra)
-    lax.fori_loop(N_DEV // GROUP // 2, N_DEV // GROUP, expand_step, 0)
-    own_copy = pltpu.make_async_copy(send_main.at[0], gmain_out.at[0], own_sem)
-    own_copy.start()
-    gextra_out[0] = send_extra[me]
-    ids_out[...] = ids_recv[...]
-
     flat[...] = jnp.zeros_like(flat)
     g_t0 = dot3(top_h, dup_h, NT_)
     for c in range(8):
@@ -400,7 +395,44 @@
     half_copy.start()
     half_copy.wait()
     own_half = flat[pl.ds(pl.multiple_of(core * HALF, HALF), HALF), :]
-    flat_out[...] = (own_half + flat_half[...]).astype(bf16)
+    flat_z[...] = (own_half + flat_half[...]).astype(bf16)
+    z_at = g // 2
+
+    def rz_copy(step):
+        to = (z_at + step) % 4
+        return pltpu.make_async_remote_copy(
+            flat_z.at[pl.ds(pl.multiple_of(to * PIECE, PIECE), PIECE)], part_z.at[step],
+            rz_ssem.at[step], rz_rsem.at[step], device_id=(to * 2 + core, m), device_id_type=MESH,
+        )
+
+    def rx_copy(step):
+        to = member_peer(step, 1)
+        return pltpu.make_async_remote_copy(
+            sum_z.at[pl.ds(pl.multiple_of(to * SMALL, SMALL), SMALL)], part_xy.at[step],
+            rx_ssem.at[step], rx_rsem.at[step], device_id=(g, to), device_id_type=MESH,
+        )
+
+    for step in range(1, 4):
+        rz_copy(step).start()
+
+    lax.fori_loop(N_DEV // GROUP // 2, N_DEV // GROUP, expand_step, 0)
+    own_copy = pltpu.make_async_copy(send_main.at[0], gmain_out.at[0], own_sem)
+    own_copy.start()
+    gextra_out[0] = send_extra[me]
+    ids_out[...] = ids_recv[...]
+
+    total = flat_z[pl.ds(pl.multiple_of(z_at * PIECE, PIECE), PIECE), :].astype(f32)
+    for step in range(1, 4):
+        rz_copy(step).wait()
+        total = total + part_z[step].astype(f32)
+    sum_z[...] = total
+    for step in range(1, N_MEMBER):
+        rx_copy(step).start()
+    total = sum_z[pl.ds(pl.multiple_of(m * SMALL, SMALL), SMALL), :]
+    for step in range(1, N_MEMBER):
+        rx_copy(step).wait()
+        total = total + part_xy[step]
+    flat_out[...] = total
 
     own_copy.wait()
     pltpu.make_async_copy(ids_send.at[pl.ds(0, 127)], ids_recv.at[pl.ds(0, 127)], ids_ssem).wait()
@@ -488,14 +520,14 @@
     return ((x + kx) % 4) * 4 + (y + ky) % 4
 
 
-CUT = (5, 9, 13)
+CUT = 5
 
 
 def parity_kernel(
     change_ref, parity_ref, flat_ref,
     new_ref, all_z,
-    pieces, part_z, sum_z, part_xy, sum_xy, all_xy,
-    ch_ssem, ch_rsem, rz_ssem, rz_rsem, rx_ssem, rx_rsem, ax_ssem, ax_rsem, az_ssem, az_rsem, ac_ssem, ac_rsem,
+    pieces, all_xy,
+    ch_ssem, ch_rsem, ax_ssem, ax_rsem, az_ssem, az_rsem, ac_ssem, ac_rsem,
 ):
     g, m = lax.axis_index("group"), lax.axis_index("member")
     barrier = pltpu.get_barrier_semaphore()
@@ -519,22 +551,8 @@
 
     z, core = g // 2, g % 2
 
-    def rz_copy(j):
-        to = (z + j) % 4
-        return remote(
-            flat_ref.at[pl.ds(pl.multiple_of(to * PIECE, PIECE), PIECE)], part_z.at[j], rz_ssem.at[j], rz_rsem.at[j],
-            (to * 2 + core, m),
-        )
-
-    def rx_copy(k):
-        to = member_peer(k, 1)
-        return remote(
-            sum_z.at[pl.ds(pl.multiple_of(to * SMALL, SMALL), SMALL)], part_xy.at[k], rx_ssem.at[k], rx_rsem.at[k],
-            (g, to),
-        )
-
     def ax_copy(k):
-        return remote(sum_xy, all_xy.at[m], ax_ssem.at[k], ax_rsem.at[k], (g, member_peer(k, 1)))
+        return remote(flat_ref, all_xy.at[m], ax_ssem.at[k], ax_rsem.at[k], (g, member_peer(k, 1)))
 
     place = core * 4 + z
 
@@ -549,36 +567,18 @@
             all_z.at[slot], all_z.at[slot], ac_ssem.at[j], ac_rsem.at[j], (z * 2 + 1 - core, m)
         )
 
-    for j in range(1, 4):
-        rz_copy(j).start()
-    for k in range(1, CUT[0]):
-        change_copy(k).start()
-    total = flat_ref[pl.ds(pl.multiple_of(z * PIECE, PIECE), PIECE), :].astype(f32)
-    for j in range(1, 4):
-        rz_copy(j).wait()
-        total = total + part_z[j].astype(f32)
-    sum_z[...] = total
-    for k in range(1, N_MEMBER):
-        rx_copy(k).start()
-    for k in range(CUT[0], CUT[1]):
-        change_copy(k).start()
-    total = sum_z[pl.ds(pl.multiple_of(m * SMALL, SMALL), SMALL), :]
-    for k in range(1, N_MEMBER):
-        rx_copy(k).wait()
-        total = total + part_xy[k]
-    sum_xy[...] = total
     for k in range(1, N_MEMBER):
         ax_copy(k).start()
-    for k in range(CUT[1], CUT[2]):
+    for k in range(1, CUT):
         change_copy(k).start()
-    all_xy[m] = total
+    all_xy[m] = flat_ref[...]
     for k in range(1, N_MEMBER):
         ax_copy(k).wait()
     all_z[place] = all_xy[...].reshape(PIECE, E).astype(bf16)
     for j in range(1, 4):
         az_copy(j).start()
     across_copy(0).start()
-    for k in range(CUT[2], N_MEMBER):
+    for k in range(CUT, N_MEMBER):
         change_copy(k).start()
 
     def weights(k):
@@ -665,7 +665,7 @@
             sds((N_DEV, 1, 128), i32),
             sds((N_DEV, MAIN, E), bf16),
             sds((N_DEV, 1, E), f32),
-            sds((HALF, E), bf16),
+            sds((SMALL, E), f32),
         ),
         in_specs=[vmem] * 5 + [anyw] * 5 + [vmem],
         out_specs=(vmem, anyw, vmem, vmem),
@@ -702,6 +702,11 @@
             VM((BOT2, E), f32),
             VM((TOPIN, TOPH), f32),
             dma((4,)),
+            VM((HALF, E), bf16),
+            VM((4, PIECE, E), bf16),
+            VM((PIECE, E), f32),
+            VM((N_MEMBER, SMALL, E), f32),
+            dma((4,)), dma((4,)), dma((N_MEMBER,)), dma((N_MEMBER,)),
         ],
         compiler_params=pltpu.CompilerParams(
             collective_id=0, has_side_effects=True, vmem_limit_bytes=56 << 20
@@ -732,12 +737,7 @@
         out_specs=(vmem, vmem),
         scratch_shapes=[
             VM((N_MEMBER, ROWS_DEV // N_MEMBER, E), bf16),
-            VM((4, PIECE, E), bf16),
-            VM((PIECE, E), f32),
             VM((N_MEMBER, SMALL, E), f32),
-            VM((SMALL, E), f32),
-            VM((N_MEMBER, SMALL, E), f32),
-            dma((N_MEMBER,)), dma((N_MEMBER,)), dma((4,)), dma((4,)),
             dma((N_MEMBER,)), dma((N_MEMBER,)), dma((N_MEMBER,)), dma((N_MEMBER,)),
             dma((4,)), dma((4,)), dma((4,)), dma((4,)),
         ],

time: 178 us -> 176 us (0.989)
  Pallas kernels: 176 us -> 174 us
    pallas_call x1, Pallas kernels: 46.1 us -> 35.5 us  [body(): pl.pallas_call(parity_kernel, out_shape=(sds(parity.shape, f32), sds((N_G...]
    pallas_call x1, Pallas kernels: 103 us -> 111 us  [body(): pl.pallas_call(exchange_kernel, out_shape=(sds((N_DEV, 1, 128), i32), sds...]
where the time goes in v5:
time: 176 us; the launch traced here: 175 us
  Pallas kernels  174 us (99%)
    pallas_call x1, Pallas kernels, body(): pl.pallas_call(exchange_kernel, out_shape=(sds((N_DEV, 1, 128), i32), sds...  111 us
    pallas_call x1, Pallas kernels, body(): pl.pallas_call(parity_kernel, out_shape=(sds(parity.shape, f32), sds((N_G...  35.5 us
    pallas_call x1, Pallas kernels, body(): pl.pallas_call(scatter_kernel, out_shape=(sds((ROWS_DEV, E), f32), sds((R...  24.3 us

profile of v5, /device:TPU:1, one launch (start us, length us, event | category | flops | bytes accessed | tf_op | source)
XLA Modules:
  0.0 174.9 jit_solution(18320571748489751671)
XLA Ops:
  0.6 111.3 %shard_map.171 = (s32[128,1,128]{2,1,0:T(1,128)}, bf16[128,96,128]{2,1,0:T(8,128)(2,1)}, f32[128,1,128]{2,1,0:T(1,128)}, f32[24,128]{1,0:T(8,128)}) custom-call(s32[64,128]{1,0:T(8,128)} %bitcast.11, s32[64,128]{1,0:T(8,128)} %bitcast.12, s32[8,128]{1,0:T(8,128)} %bitcast.14, f32[13,128]{1,0:T(8,128)} %bitcast.13, f32[1,128]{1,0:T(1,128)} %bitcast.16, ...), custom_call_target="tpu_custom_call" | custom-call | tf_op jit(solution)/shard_map/pallas_call | solution.py:662
  111.9 24.3 %shard_map.172 = (f32[8192,128]{1,0:T(8,128)}, bf16[8192,128]{1,0:T(8,128)(2,1)}) custom-call(s32[128,1,128]{2,1,0:T(1,128)} %get-tuple-element.21.ids_ref, bf16[128,96,128]{2,1,0:T(8,128)(2,1)} %get-tuple-element.22.gmain_hbm, f32[128,1,128]{2,1,0:T(1,128)} %get-tuple-element.23.gextra_ref, f32[8192,128]{1,0:T(8,128)} %table_hbm.3), custom_call_target="tpu_custom_call" | custom-call | tf_op jit(solution)/shard_map/pallas_call | solution.py:718
  136.2 35.5 %shard_map.173 = (f32[512,256]{1,0:T(8,128)}, bf16[8,384,128]{2,1,0:T(8,128)(2,1)}) custom-call(bf16[8192,128]{1,0:T(8,128)(2,1)} %get-tuple-element.25.change_ref, f32[512,256]{1,0:T(8,128)} %parity_ref.1, f32[24,128]{1,0:T(8,128)} %get-tuple-element.26.flat_ref), custom_call_target="tpu_custom_call" | custom-call | tf_op jit(solution)/shard_map/pallas_call | solution.py:733
  171.8 2.9 %shard_map.174 = (f32[512,256]{1,0:T(8,128)}, f32[13,512]{1,0:T(8,128)}, f32[512,256]{1,0:T(8,128)}, f32[256,128]{1,0:T(8,128)}, f32[164,1024]{1,0:T(8,128)}, /*index=5*/f32[1,1024]{1,0:T(1,128)}) custom-call(f32[512,256]{1,0:T(8,128)} %get-tuple-element.27.parity_hbm, bf16[8,384,128]{2,1,0:T(8,128)(2,1)} %get-tuple-element.28.all_z_hbm), custom_call_target="tpu_custom_call" | custom-call | tf_op jit(solution)/shard_map/pallas_call | solution.py:748

commit v6 on v4

--- a/solution.py
+++ b/solution.py
@@ -495,7 +495,7 @@
     change_ref, parity_ref, flat_ref,
     new_ref, all_z,
     pieces, part_z, sum_z, part_xy, sum_xy, all_xy,
-    ch_ssem, ch_rsem, rz_ssem, rz_rsem, rx_ssem, rx_rsem, ax_ssem, ax_rsem, az_ssem, az_rsem, ac_ssem, ac_rsem,
+    ch_ssem, ch_rsem, rz_ssem, rz_rsem, rx_ssem, rx_rsem, ax_ssem, ax_rsem, az_ssem, az_rsem, ac_ssem, ac_rsem, own_sem,
 ):
     g, m = lax.axis_index("group"), lax.axis_index("member")
     barrier = pltpu.get_barrier_semaphore()
@@ -549,6 +549,10 @@
             all_z.at[slot], all_z.at[slot], ac_ssem.at[j], ac_rsem.at[j], (z * 2 + 1 - core, m)
         )
 
+    own_copy = pltpu.make_async_copy(
+        change_ref.at[pl.ds(pl.multiple_of(m * rows, rows), rows)], pieces.at[0], own_sem
+    )
+    own_copy.start()
     for j in range(1, 4):
         rz_copy(j).start()
     for k in range(1, CUT[0]):
@@ -602,7 +606,8 @@
 
         lax.fori_loop(0, rows // 64, step, 0)
 
-    add(0, lambda b: change_ref[pl.ds(pl.multiple_of(m * rows + b * 64, 64), 64), :], parity_ref)
+    own_copy.wait()
+    add(0, lambda b: pieces[0, pl.ds(pl.multiple_of(b * 64, 64), 64), :], parity_ref)
     for k in range(1, N_MEMBER):
         change_copy(k).wait()
         add(k, lambda b: pieces[k, pl.ds(pl.multiple_of(b * 64, 64), 64), :], new_ref)
@@ -728,7 +733,7 @@
     parity_sum, all_z = pl.pallas_call(
         parity_kernel,
         out_shape=(sds(parity.shape, f32), sds((N_GROUP, PIECE, E), bf16)),
-        in_specs=[vmem] * 3,
+        in_specs=[anyw, vmem, vmem],
         out_specs=(vmem, vmem),
         scratch_shapes=[
             VM((N_MEMBER, ROWS_DEV // N_MEMBER, E), bf16),
@@ -739,10 +744,10 @@
             VM((N_MEMBER, SMALL, E), f32),
             dma((N_MEMBER,)), dma((N_MEMBER,)), dma((4,)), dma((4,)),
             dma((N_MEMBER,)), dma((N_MEMBER,)), dma((N_MEMBER,)), dma((N_MEMBER,)),
-            dma((4,)), dma((4,)), dma((4,)), dma((4,)),
+            dma((4,)), dma((4,)), dma((4,)), dma((4,)), dma,
         ],
         compiler_params=pltpu.CompilerParams(
-            collective_id=1, has_side_effects=True, vmem_limit_bytes=56 << 20
+            collective_id=1, has_side_effects=True, vmem_limit_bytes=60 << 20
         ),
     )(change, parity, flat)
     new_parity, g0, g1, g2, gt0, gt1 = pl.pallas_call(

time: 178 us -> 178 us (level)
  no operation moved by 1% of the time
where the time goes in v6:
time: 178 us; the launch traced here: 176 us
  Pallas kernels  175 us (98%)
    pallas_call x1, Pallas kernels, body(): pl.pallas_call(exchange_kernel, out_shape=(sds((N_DEV, 1, 128), i32), sds...  103 us
    pallas_call x1, Pallas kernels, body(): pl.pallas_call(parity_kernel, out_shape=(sds(parity.shape, f32), sds((N_G...  45 us
    pallas_call x1, Pallas kernels, body(): pl.pallas_call(scatter_kernel, out_shape=(sds((ROWS_DEV, E), f32), sds((R...  24.1 us

profile of v6, /device:TPU:1, one launch (start us, length us, event | category | flops | bytes accessed | tf_op | source)
XLA Modules:
  0.0 175.9 jit_solution(7474017248117962730)
XLA Ops:
  0.6 103.0 %shard_map.171 = (s32[128,1,128]{2,1,0:T(1,128)}, bf16[128,96,128]{2,1,0:T(8,128)(2,1)}, f32[128,1,128]{2,1,0:T(1,128)}, bf16[1536,128]{1,0:T(8,128)(2,1)}) custom-call(s32[64,128]{1,0:T(8,128)} %bitcast.11, s32[64,128]{1,0:T(8,128)} %bitcast.12, s32[8,128]{1,0:T(8,128)} %bitcast.14, f32[13,128]{1,0:T(8,128)} %bitcast.13, f32[1,128]{1,0:T(1,128)} %bitcast.16, ...), custom_call_target="tpu_custom_call" | custom-call | tf_op jit(solution)/shard_map/pallas_call | solution.py:667
  103.7 24.1 %shard_map.172 = (f32[8192,128]{1,0:T(8,128)}, bf16[8192,128]{1,0:T(8,128)(2,1)}) custom-call(s32[128,1,128]{2,1,0:T(1,128)} %get-tuple-element.21.ids_ref, bf16[128,96,128]{2,1,0:T(8,128)(2,1)} %get-tuple-element.22.gmain_hbm, f32[128,1,128]{2,1,0:T(1,128)} %get-tuple-element.23.gextra_ref, f32[8192,128]{1,0:T(8,128)} %table_hbm.3), custom_call_target="tpu_custom_call" | custom-call | tf_op jit(solution)/shard_map/pallas_call | solution.py:718
  127.8 45.0 %shard_map.173 = (f32[512,256]{1,0:T(8,128)}, bf16[8,384,128]{2,1,0:T(8,128)(2,1)}) custom-call(bf16[8192,128]{1,0:T(8,128)(2,1)} %get-tuple-element.25.change_ref, f32[512,256]{1,0:T(8,128)} %parity_ref.1, bf16[1536,128]{1,0:T(8,128)(2,1)} %get-tuple-element.26.flat_ref), custom_call_target="tpu_custom_call" | custom-call | tf_op jit(solution)/shard_map/pallas_call | solution.py:733
  172.8 2.9 %shard_map.174 = (f32[512,256]{1,0:T(8,128)}, f32[13,512]{1,0:T(8,128)}, f32[512,256]{1,0:T(8,128)}, f32[256,128]{1,0:T(8,128)}, f32[164,1024]{1,0:T(8,128)}, /*index=5*/f32[1,1024]{1,0:T(1,128)}) custom-call(f32[512,256]{1,0:T(8,128)} %get-tuple-element.27.parity_hbm, bf16[8,384,128]{2,1,0:T(8,128)(2,1)} %get-tuple-element.28.all_z_hbm), custom_call_target="tpu_custom_call" | custom-call | tf_op jit(solution)/shard_map/pallas_call | solution.py:753
